TPU v7x, 128 devices: a whole 4x4x4 slice. The times are simulated.
128 devices in a mesh: blank: 8 (over z, core), tool: 16 (over x, y).
Axes of the slice: x: 4, y: 4, z: 4, core: 2. Of those that a mesh axis runs over, the one named last changes fastest.
Arguments:
- tool_temp: float32 [128, 512, 1024], P('tool', 'blank'), may hold values from -6 to 6
- material: int32 [128, 512, 1024], P('tool', 'blank'), may hold values from 0 to 7
- conductivity: float32 [8], replicated, may hold values from 0.15 to 1.3
- shell_temp: float32 [65536, 128], P(('blank', 'tool')), may hold values from -6 to 6
- base_rate: float32 [65536, 128], P(('blank', 'tool')), may hold values from 0.1 to 1
- film: float32 [65536, 128], P(('blank', 'tool')), may hold values from 0.2 to 2
- contact_temp: float32 [65536, 128], P(('blank', 'tool')), may hold values from -6 to 6
- pair_slab: int32 [65536, 1], P(('blank', 'tool')), may hold values from 0 to 15; in each aligned block of 512 rows (0 to 511, 512 to 1023, ...) at most 64 rows name the same one
- pair_block: int32 [65536], P(('blank', 'tool')), may hold values from 0 to 4095
- bead_ids: int32 [524288], P(('blank', 'tool')), may hold values from 0 to 65535
- bead_gain: float32 [524288], P(('blank', 'tool')), may hold values from 0.5 to 2
Outputs:
- tool_out: float32 [128, 512, 1024], P('tool', 'blank')
- shell_out: float32 [65536, 128], P(('blank', 'tool'))
- contact_out: float32 [65536, 128], P(('blank', 'tool'))
Inputs may be any that keep to these rules, and one draw needn't show every extreme that they name: `pair_slab`: in the 512 rows of one device no slab is named more than 64 times, a bound that some block reaches.
All inputs are finite; a program needn't handle non-finite values.
Results may differ from a plain program's by a relative error of at most 0.00002.
Values sent between devices are 32-bit elements; how exact they have to be, the bound alone decides.
A program may use at most 192 MiB of HBM per device.

v0:
```python
import jax
import jax.numpy as jnp
from jax import lax
from jax.sharding import PartitionSpec as P

STEPS = 2
SWEEPS = 4


diffuse_step = 0.12
source_step = 0.25
shell_step = 0.5


def with_halo(block, sides, width):
    for axis, dim in sides:
        count = lax.axis_size(axis)
        forward = [(i, i + 1) for i in range(count - 1)]
        backward = [(target, source) for source, target in forward]
        low = lax.ppermute(
            lax.slice_in_dim(block, block.shape[dim] - width, None, axis=dim), axis, forward
        )
        high = lax.ppermute(lax.slice_in_dim(block, 0, width, axis=dim), axis, backward)
        block = jnp.concatenate([low, block, high], axis=dim)
    return block


def offsets():
    return [(2, 1, 1), (0, 1, 1), (1, 2, 1), (1, 0, 1), (1, 1, 2), (1, 1, 0)]


def window(padded, shift, shape):
    return lax.slice(padded, shift, (shift[0] + shape[0], shift[1] + shape[1], shift[2] + shape[2]))


def face_list(kpad, shape):
    center = kpad[1:-1, 1:-1, 1:-1]
    return [0.5 * (center + window(kpad, shift, shape)) for shift in offsets()]


def on_device(
    tool_temp,
    material,
    conductivity,
    shell_temp,
    base_rate,
    film,
    contact_temp,
    pair_slab,
    pair_block,
    bead_ids,
    bead_gain,
):
    shape = tool_temp.shape
    blocks = shell_temp.shape[0]
    nblocks = shape[0] * shape[1] * shape[2] // 128
    kfield = jnp.zeros(shape, jnp.float32)
    for mat in range(conductivity.shape[0]):
        kfield = jnp.where(material == mat, conductivity[mat], kfield)
    krim = with_halo(kfield, (("blank", 1), ("tool", 0)), 1)
    kpad = jnp.pad(krim, ((0, 0), (0, 0), (1, 1)))
    faces = face_list(kpad, shape)
    slab = pair_slab[:, 0]
    theta = shell_temp
    iface = contact_temp
    field = tool_temp
    for step in range(STEPS):
        flux = film * (iface - theta)
        sigma = 1.0 - 0.4 * jnp.tanh(theta)
        force = bead_gain * sigma.reshape(-1)[bead_ids]
        extra = jnp.zeros((blocks * 128,), jnp.float32).at[bead_ids].add(force)
        rate = base_rate + extra.reshape(blocks, 128)
        outflow = -flux
        rows_all, slab_all, block_all = (
            lax.all_gather(outflow, "tool", axis=0, tiled=True),
            lax.all_gather(slab, "tool", axis=0, tiled=True),
            lax.all_gather(pair_block, "tool", axis=0, tiled=True),
        )
        mine = slab_all == lax.axis_index("tool")
        target = jnp.where(mine, block_all, 0)
        source = (
            jnp.zeros((nblocks, 128), jnp.float32)
            .at[target]
            .add(jnp.where(mine[:, None], rows_all, 0.0))
        )
        theta = theta + shell_step * (flux + sigma * rate)
        source = source.reshape(shape)
        for sweep_idx in range(SWEEPS):
            rim = with_halo(field, (("blank", 1), ("tool", 0)), 1)
            padded = jnp.pad(rim, ((0, 0), (0, 0), (1, 1)))
            total = jnp.zeros(shape, jnp.float32)
            for face, shift in zip(faces, offsets()):
                total = total + face * (window(padded, shift, shape) - field)
            field = field + diffuse_step * total + source_step * source
        field_blocks = field.reshape(nblocks, 128)
        values = jnp.where(mine[:, None], field_blocks[target], 0.0)
        iface = lax.psum_scatter(values, "tool", scatter_dimension=0, tiled=True)
    return (field, theta, iface)


def solution(mesh):
    placed = (
        P("tool", "blank", None),
        P("tool", "blank", None),
        P(),
        P(("blank", "tool"), None),
        P(("blank", "tool"), None),
        P(("blank", "tool"), None),
        P(("blank", "tool"), None),
        P(("blank", "tool"), None),
        P(("blank", "tool")),
        P(("blank", "tool")),
        P(("blank", "tool")),
    )
    return jax.shard_map(
        on_device,
        mesh=mesh,
        in_specs=placed,
        out_specs=(
            P("tool", "blank", None),
            P(("blank", "tool"), None),
            P(("blank", "tool"), None),
        ),
        check_vma=False,
    )
```

profile of v0, /device:TPU:96, one launch (start us, length us, event | category | flops | bytes accessed | tf_op | source)
XLA Modules:
  0.0 775.2 jit_solution(5534686494707768519)
XLA Ops:
  9.0 23.0 %gather_fusion.1 = f32[4096]{0:T(1024)S(1)} fusion(f32[65536]{0:T(1024)S(1)} %fusion.174, s32[4096]{0:T(1024)S(1)} %get-tuple-element.49), kind=kCustom, calls=%fused_computation.1 | custom fusion | bytes 49152 | tf_op jit(solution)/shard_map/gather | solution.py:70
  32.1 22.0 %scatter_custom_fusion.1 = f32[65536]{0:T(1024)S(1)} fusion(s32[4096]{0:T(1024)S(1)} %get-tuple-element.50, f32[4096]{0:T(1024)S(1)} %mul.279, f32[]{:T(128)} %constant.2.clone.1), kind=kCustom, calls=%fused_computation.351 | custom fusion | flops 4096 | bytes 262148 | tf_op jit(solution)/shard_map/scatter-add | solution.py:71
  62.5 7.7 select_select_fusion
  75.8 23.8 %all-gather = s32[8192,1]{0,1:T(1,128)S(1)} all-gather(s32[512,1]{0,1:T(1,128)S(1)} %copy-done.26), channel_id=2, replica_groups=mesh['blank'=8,'tool'=16] {'tool'}, dimensions={0}, use_global_device_ids=true | all-gather | bytes 34816 | tf_op jit(solution)/shard_map/all_gather | solution.py:76
  99.7 22.9 %all-gather.1 = s32[16,1,512]{2,1,0:T(1,128)S(1)} all-gather(s32[1,1,512]{2,1,0:T(1,128)S(1)} %bitcast.36), channel_id=1, replica_groups=mesh['blank'=8,'tool'=16] {'tool'}, dimensions={0}, use_global_device_ids=true | all-gather | bytes 34816 | tf_op jit(solution)/shard_map/all_gather | solution.py:77
  126.0 4.6 collective-permute-start.7
  144.0 59.5 %scatter_custom_fusion = f32[4096,128]{1,0:T(8,128)} fusion(s32[8192]{0:T(1024)S(1)} %get-tuple-element.6, f32[8192,128]{1,0:T(8,128)} %all-gather.5.cloned.1.call-done, f32[]{:T(128)} %constant.2.clone.1, pred[8192]{0:T(1024)(128)(4,1)S(1)} %compare_reduce_fusion), kind=kCustom, calls=%fused_computation.12 | custom fusion | flops 2097152 | bytes 6300672 | tf_op jit(solution)/shard_map/scatter-add | solution.py:84
  209.3 11.5 %fusion.135 = (f32[8,64,1024]{2,1,0:T(8,128)S(1)}, f32[8,64,1024]{2,1,0:T(8,128)S(1)}, f32[8,64,1024]{2,1,0:T(8,128)S(1)}) fusion(f32[8,64,1024]{2,1,0:T(8,128)} %mul.249, f32[8,64,1024]{2,1,0:T(8,128)} %param.11, f32[10,66,1026]{2,1,0:T(8,128)} %select_maximum_fusion.28, f32[8,1,1024]{2,1,0:T(1,128)S(1)} %collective-permute-done.3, ...), kind=kLoop, calls=%fused_computation.252 | loop fusion | flops 25165824 | bytes 22183936 | tf_op jit(solution)/shard_map/add | solution.py:94
  228.1 4.6 collective-permute-start.11
  237.2 5.7 collective-permute-done.10
  245.8 4.5 fusion.117
  252.3 5.0 collective-permute-start.13
  258.9 6.3 collective-permute-start.15
  283.1 5.7 collective-permute-start.17
  306.2 5.3 fusion.81
  313.2 27.7 %gather_fusion = f32[8192,128]{1,0:T(8,128)} fusion(f32[4096,128]{1,0:T(8,128)S(1)} %reshape.31, s32[8192]{0:T(1024)S(1)} %get-tuple-element.5), kind=kCustom, calls=%fused_computation | custom fusion | bytes 8421376 | tf_op jit(solution)/shard_map/gather | solution.py:96
  340.9 7.5 broadcast_select_fusion.1
  349.1 40.5 %gather_fusion.2 = f32[4096]{0:T(1024)} fusion(f32[65536]{0:T(1024)S(1)} %get-tuple-element.3, s32[4096]{0:T(1024)S(1)} %copy-done.21), kind=kCustom, calls=%fused_computation.2 | custom fusion | bytes 49152 | tf_op jit(solution)/shard_map/gather | solution.py:70
  391.1 22.1 %scatter_custom_fusion.3 = f32[65536]{0:T(1024)S(1)} fusion(s32[4096]{0:T(1024)} %copy-done.25, f32[4096]{0:T(1024)} %mul.307, f32[]{:T(128)} %constant.2.clone.1), kind=kCustom, calls=%fused_computation.349 | custom fusion | flops 4096 | bytes 262656 | tf_op jit(solution)/shard_map/scatter-add | solution.py:71
  413.2 16.8 %reduce-scatter.3.cloned.1.call-done = f32[512,128]{1,0:T(8,128)} async-done(((f32[8192,128]{1,0:T(8,128)}), f32[512,128]{1,0:T(8,128)}) %reduce-scatter.3.cloned.1.call-update) | async-done | bytes 262160 | tf_op jit(solution)/shard_map/reduce_scatter | solution.py:97
  443.8 5.7 collective-permute-done.23
  449.5 5.0 collective-permute-done.22
  459.3 29.2 %all-gather.7.cloned.1.call-done = f32[8192,128]{1,0:T(8,128)} async-done(((f32[512,128]{1,0:T(8,128)}), f32[8192,128]{1,0:T(8,128)}) %all-gather.7.cloned.1.call-update) | async-done | bytes 4194320 | tf_op jit(solution)/shard_map/all_gather | solution.py:75
  488.5 58.7 %scatter_custom_fusion.2 = f32[4096,128]{1,0:T(8,128)S(1)} fusion(s32[8192]{0:T(1024)} %copy-done.23, f32[8192,128]{1,0:T(8,128)} %all-gather.7.cloned.1.call-done, f32[]{:T(128)} %constant.2.clone.1, pred[8192]{0:T(1024)(128)(4,1)S(1)} %compare_reduce_fusion), kind=kCustom, calls=%fused_computation.10 | custom fusion | flops 2097152 | bytes 6300672 | tf_op jit(solution)/shard_map/scatter-add | solution.py:84
  551.6 10.4 %fusion.63 = f32[8,64,1024]{2,1,0:T(8,128)S(1)} fusion(f32[8,64,1024]{2,1,0:T(8,128)} %mul.284, f32[8,64,1024]{2,1,0:T(8,128)} %fusion.81, f32[8,64,1024]{2,1,0:T(8,128)} %copy-done.4, f32[10,66,1026]{2,1,0:T(8,128)} %select_maximum_fusion.12, f32[8,64,1024]{2,1,0:T(8,128)} %copy-done.2, f32[8,1,1024]{2,1,0:T(1,128)S(1)} %collective-permute-done.20, ...), kind=kLoop, calls=%fused_computation.140 | loop fusion | flops 23068672 | bytes 17989632 | tf_op jit(solution)/shard_map/add | solution.py:94
  569.2 4.9 collective-permute-start.27
  592.4 5.2 collective-permute-start.29
  621.1 4.5 collective-permute-start.33
  643.2 5.3 fusion.9
  650.2 27.7 %gather_fusion.3 = f32[8192,128]{1,0:T(8,128)} fusion(f32[4096,128]{1,0:T(8,128)S(1)} %reshape.36, s32[8192]{0:T(1024)S(1)} %copy-done.18), kind=kCustom, calls=%fused_computation.3 | custom fusion | bytes 8421376 | tf_op jit(solution)/shard_map/gather | solution.py:96
  677.8 7.5 broadcast_select_fusion
  685.3 82.8 %reduce-scatter.5.cloned.1.call-done = f32[512,128]{1,0:T(8,128)} async-done(((f32[8192,128]{1,0:T(8,128)}), f32[512,128]{1,0:T(8,128)}) %reduce-scatter.5.cloned.1.call-update) | async-done | bytes 262160 | tf_op jit(solution)/shard_map/reduce_scatter | solution.py:97
  (171 shorter events, 186.6 us)
Async XLA Ops:
  7.2 136.9 %all-gather.5.cloned.1.call-start = ((), (), s32[]{:S(2)}) async-start(), calls=%async_computation.2 | async-start | bytes 4456448 | tf_op jit(solution)/shard_map/all_gather | solution.py:75
  55.1 375.0 %reduce-scatter.3.cloned.1.call-start = ((), (), s32[]{:S(2)}) async-start(), calls=%async_computation.3 | async-start | bytes 4456448 | tf_op jit(solution)/shard_map/reduce_scatter | solution.py:97
  56.2 69.7 %collective-permute-start.3 = (f32[8,1,1024]{2,1,0:T(1,128)S(1)}, f32[8,1,1024]{2,1,0:T(1,128)S(1)}, u32[]{:S(2)}, u32[]{:S(2)}) collective-permute-start(f32[8,1,1024]{2,1,0:T(1,128)S(1)} %get-tuple-element.44), channel_id=1, source_target_pairs={{0,16},{16,32},{32,48},{48,64},{64,80},{80,96},{96,112},{1,17},{17... | collective-permute-start | bytes 98312 | tf_op jit(solution)/shard_map/ppermute | solution.py:20
  58.1 67.8 %collective-permute-start.4 = (f32[8,1,1024]{2,1,0:T(1,128)S(1)}, f32[8,1,1024]{2,1,0:T(1,128)S(1)}, u32[]{:S(2)}, u32[]{:S(2)}) collective-permute-start(f32[8,1,1024]{2,1,0:T(1,128)S(1)} %get-tuple-element.45), channel_id=1, source_target_pairs={{16,0},{32,16},{48,32},{64,48},{80,64},{96,80},{112,96},{17,1},{33... | collective-permute-start | bytes 98312 | tf_op jit(solution)/shard_map/ppermute | solution.py:23
  70.2 52.4 %collective-permute-start = (f32[8,1,1024]{2,1,0:T(1,128)S(1)}, f32[8,1,1024]{2,1,0:T(1,128)S(1)}, u32[]{:S(2)}, u32[]{:S(2)}) collective-permute-start(f32[8,1,1024]{2,1,0:T(1,128)S(1)} %get-tuple-element.42), channel_id=1, source_target_pairs={{0,16},{16,32},{32,48},{48,64},{64,80},{80,96},{96,112},{1,17},{17... | collective-permute-start | bytes 98312 | tf_op jit(solution)/shard_map/ppermute | solution.py:20
  72.1 50.4 %collective-permute-start.1 = (f32[8,1,1024]{2,1,0:T(1,128)S(1)}, f32[8,1,1024]{2,1,0:T(1,128)S(1)}, u32[]{:S(2)}, u32[]{:S(2)}) collective-permute-start(f32[8,1,1024]{2,1,0:T(1,128)S(1)} %get-tuple-element.43), channel_id=1, source_target_pairs={{16,0},{32,16},{48,32},{64,48},{80,64},{96,80},{112,96},{17,1},{33... | collective-permute-start | bytes 98312 | tf_op jit(solution)/shard_map/ppermute | solution.py:23
  122.7 9.3 %collective-permute-start.6 = (f32[1,66,1024]{2,1,0:T(8,128)S(1)}, f32[1,66,1024]{2,1,0:T(8,128)S(1)}, u32[]{:S(2)}, u32[]{:S(2)}) collective-permute-start(f32[1,66,1024]{2,1,0:T(8,128)S(1)} %get-tuple-element.24), channel_id=1, source_target_pairs={{0,1},{1,2},{2,3},{3,4},{4,5},{5,6},{6,7},{7,8},{8,9},{9,10},{10,1... | collective-permute-start | bytes 811016 | tf_op jit(solution)/shard_map/ppermute | solution.py:20
  124.6 8.6 %collective-permute-start.2 = (f32[1,66,1024]{2,1,0:T(8,128)S(1)}, f32[1,66,1024]{2,1,0:T(8,128)S(1)}, u32[]{:S(2)}, u32[]{:S(2)}) collective-permute-start(f32[1,66,1024]{2,1,0:T(8,128)S(1)} %get-tuple-element.25), channel_id=1, source_target_pairs={{1,0},{2,1},{3,2},{4,3},{5,4},{6,5},{7,6},{8,7},{9,8},{10,9},{11,1... | collective-permute-start | bytes 811016 | tf_op jit(solution)/shard_map/ppermute | solution.py:23
  126.0 11.2 %collective-permute-start.7 = (f32[1,66,1024]{2,1,0:T(8,128)S(1)}, f32[1,66,1024]{2,1,0:T(8,128)S(1)}, u32[]{:S(2)}, u32[]{:S(2)}) collective-permute-start(f32[1,66,1024]{2,1,0:T(8,128)S(1)} %get-tuple-element.26), channel_id=1, source_target_pairs={{0,1},{1,2},{2,3},{3,4},{4,5},{5,6},{6,7},{7,8},{8,9},{9,10},{10,1... | collective-permute-start | bytes 811016 | tf_op jit(solution)/shard_map/ppermute | solution.py:20
  130.6 8.6 %collective-permute-start.5 = (f32[1,66,1024]{2,1,0:T(8,128)S(1)}, f32[1,66,1024]{2,1,0:T(8,128)S(1)}, u32[]{:S(2)}, u32[]{:S(2)}) collective-permute-start(f32[1,66,1024]{2,1,0:T(8,128)S(1)} %get-tuple-element.27), channel_id=1, source_target_pairs={{1,0},{2,1},{3,2},{4,3},{5,4},{6,5},{7,6},{8,7},{9,8},{10,9},{11,1... | collective-permute-start | bytes 811016 | tf_op jit(solution)/shard_map/ppermute | solution.py:23
  228.1 9.1 %collective-permute-start.11 = (f32[1,66,1024]{2,1,0:T(8,128)S(1)}, f32[1,66,1024]{2,1,0:T(8,128)S(1)}, u32[]{:S(2)}, u32[]{:S(2)}) collective-permute-start(f32[1,66,1024]{2,1,0:T(8,128)S(1)} %get-tuple-element.22), channel_id=1, source_target_pairs={{0,1},{1,2},{2,3},{3,4},{4,5},{5,6},{6,7},{7,8},{8,9},{9,10},{10,1... | collective-permute-start | bytes 811016 | tf_op jit(solution)/shard_map/ppermute | solution.py:20
  232.8 10.1 %collective-permute-start.10 = (f32[1,66,1024]{2,1,0:T(8,128)S(1)}, f32[1,66,1024]{2,1,0:T(8,128)S(1)}, u32[]{:S(2)}, u32[]{:S(2)}) collective-permute-start(f32[1,66,1024]{2,1,0:T(8,128)S(1)} %get-tuple-element.23), channel_id=1, source_target_pairs={{1,0},{2,1},{3,2},{4,3},{5,4},{6,5},{7,6},{8,7},{9,8},{10,9},{11,1... | collective-permute-start | bytes 811016 | tf_op jit(solution)/shard_map/ppermute | solution.py:23
  250.3 6.9 collective-permute-start.12
  252.3 6.6 collective-permute-start.13
  258.9 10.5 %collective-permute-start.15 = (f32[1,66,1024]{2,1,0:T(8,128)S(1)}, f32[1,66,1024]{2,1,0:T(8,128)S(1)}, u32[]{:S(2)}, u32[]{:S(2)}) collective-permute-start(f32[1,66,1024]{2,1,0:T(8,128)S(1)} %get-tuple-element.20), channel_id=1, source_target_pairs={{0,1},{1,2},{2,3},{3,4},{4,5},{5,6},{6,7},{7,8},{8,9},{9,10},{10,1... | collective-permute-start | bytes 811016 | tf_op jit(solution)/shard_map/ppermute | solution.py:20
  265.2 8.6 %collective-permute-start.14 = (f32[1,66,1024]{2,1,0:T(8,128)S(1)}, f32[1,66,1024]{2,1,0:T(8,128)S(1)}, u32[]{:S(2)}, u32[]{:S(2)}) collective-permute-start(f32[1,66,1024]{2,1,0:T(8,128)S(1)} %get-tuple-element.21), channel_id=1, source_target_pairs={{1,0},{2,1},{3,2},{4,3},{5,4},{6,5},{7,6},{8,7},{9,8},{10,9},{11,1... | collective-permute-start | bytes 811016 | tf_op jit(solution)/shard_map/ppermute | solution.py:23
  281.2 7.7 collective-permute-start.16
  283.1 7.3 collective-permute-start.17
  290.5 8.4 %collective-permute-start.19 = (f32[1,66,1024]{2,1,0:T(8,128)S(1)}, f32[1,66,1024]{2,1,0:T(8,128)S(1)}, u32[]{:S(2)}, u32[]{:S(2)}) collective-permute-start(f32[1,66,1024]{2,1,0:T(8,128)S(1)} %get-tuple-element.18), channel_id=1, source_target_pairs={{0,1},{1,2},{2,3},{3,4},{4,5},{5,6},{6,7},{7,8},{8,9},{9,10},{10,1... | collective-permute-start | bytes 811016 | tf_op jit(solution)/shard_map/ppermute | solution.py:20
  294.7 8.6 %collective-permute-start.18 = (f32[1,66,1024]{2,1,0:T(8,128)S(1)}, f32[1,66,1024]{2,1,0:T(8,128)S(1)}, u32[]{:S(2)}, u32[]{:S(2)}) collective-permute-start(f32[1,66,1024]{2,1,0:T(8,128)S(1)} %get-tuple-element.19), channel_id=1, source_target_pairs={{1,0},{2,1},{3,2},{4,3},{5,4},{6,5},{7,6},{8,7},{9,8},{10,9},{11,1... | collective-permute-start | bytes 811016 | tf_op jit(solution)/shard_map/ppermute | solution.py:23
  348.4 140.1 %all-gather.7.cloned.1.call-start = ((), (), s32[]{:S(2)}) async-start(), calls=%async_computation.4 | async-start | bytes 4456448 | tf_op jit(solution)/shard_map/all_gather | solution.py:75
  432.0 336.1 %reduce-scatter.5.cloned.1.call-start = ((), (), s32[]{:S(2)}) async-start(), calls=%async_computation.5 | async-start | bytes 4456448 | tf_op jit(solution)/shard_map/reduce_scatter | solution.py:97
  439.4 10.1 %collective-permute-start.23 = (f32[1,66,1024]{2,1,0:T(8,128)S(1)}, f32[1,66,1024]{2,1,0:T(8,128)S(1)}, u32[]{:S(2)}, u32[]{:S(2)}) collective-permute-start(f32[1,66,1024]{2,1,0:T(8,128)S(1)} %get-tuple-element.16), channel_id=1, source_target_pairs={{0,1},{1,2},{2,3},{3,4},{4,5},{5,6},{6,7},{7,8},{8,9},{9,10},{10,1... | collective-permute-start | bytes 811016 | tf_op jit(solution)/shard_map/ppermute | solution.py:20
  442.5 11.9 %collective-permute-start.22 = (f32[1,66,1024]{2,1,0:T(8,128)S(1)}, f32[1,66,1024]{2,1,0:T(8,128)S(1)}, u32[]{:S(2)}, u32[]{:S(2)}) collective-permute-start(f32[1,66,1024]{2,1,0:T(8,128)S(1)} %get-tuple-element.17), channel_id=1, source_target_pairs={{1,0},{2,1},{3,2},{4,3},{5,4},{6,5},{7,6},{8,7},{9,8},{10,9},{11,1... | collective-permute-start | bytes 811016 | tf_op jit(solution)/shard_map/ppermute | solution.py:23
  569.2 9.4 %collective-permute-start.27 = (f32[1,66,1024]{2,1,0:T(8,128)S(1)}, f32[1,66,1024]{2,1,0:T(8,128)S(1)}, u32[]{:S(2)}, u32[]{:S(2)}) collective-permute-start(f32[1,66,1024]{2,1,0:T(8,128)S(1)} %get-tuple-element.14), channel_id=1, source_target_pairs={{0,1},{1,2},{2,3},{3,4},{4,5},{5,6},{6,7},{7,8},{8,9},{9,10},{10,1... | collective-permute-start | bytes 811016 | tf_op jit(solution)/shard_map/ppermute | solution.py:20
  574.1 8.9 %collective-permute-start.26 = (f32[1,66,1024]{2,1,0:T(8,128)S(1)}, f32[1,66,1024]{2,1,0:T(8,128)S(1)}, u32[]{:S(2)}, u32[]{:S(2)}) collective-permute-start(f32[1,66,1024]{2,1,0:T(8,128)S(1)} %get-tuple-element.15), channel_id=1, source_target_pairs={{1,0},{2,1},{3,2},{4,3},{5,4},{6,5},{7,6},{8,7},{9,8},{10,9},{11,1... | collective-permute-start | bytes 811016 | tf_op jit(solution)/shard_map/ppermute | solution.py:23
  590.5 7.1 collective-permute-start.28
  592.4 6.8 collective-permute-start.29
  599.2 8.1 %collective-permute-start.31 = (f32[1,66,1024]{2,1,0:T(8,128)S(1)}, f32[1,66,1024]{2,1,0:T(8,128)S(1)}, u32[]{:S(2)}, u32[]{:S(2)}) collective-permute-start(f32[1,66,1024]{2,1,0:T(8,128)S(1)} %get-tuple-element.12), channel_id=1, source_target_pairs={{0,1},{1,2},{2,3},{3,4},{4,5},{5,6},{6,7},{7,8},{8,9},{9,10},{10,1... | collective-permute-start | bytes 811016 | tf_op jit(solution)/shard_map/ppermute | solution.py:20
  603.1 8.6 %collective-permute-start.30 = (f32[1,66,1024]{2,1,0:T(8,128)S(1)}, f32[1,66,1024]{2,1,0:T(8,128)S(1)}, u32[]{:S(2)}, u32[]{:S(2)}) collective-permute-start(f32[1,66,1024]{2,1,0:T(8,128)S(1)} %get-tuple-element.13), channel_id=1, source_target_pairs={{1,0},{2,1},{3,2},{4,3},{5,4},{6,5},{7,6},{8,7},{9,8},{10,9},{11,1... | collective-permute-start | bytes 811016 | tf_op jit(solution)/shard_map/ppermute | solution.py:23
  627.3 8.6 %collective-permute-start.35 = (f32[1,66,1024]{2,1,0:T(8,128)S(1)}, f32[1,66,1024]{2,1,0:T(8,128)S(1)}, u32[]{:S(2)}, u32[]{:S(2)}) collective-permute-start(f32[1,66,1024]{2,1,0:T(8,128)S(1)} %get-tuple-element.10), channel_id=1, source_target_pairs={{0,1},{1,2},{2,3},{3,4},{4,5},{5,6},{6,7},{7,8},{8,9},{9,10},{10,1... | collective-permute-start | bytes 811016 | tf_op jit(solution)/shard_map/ppermute | solution.py:20
  631.7 8.6 %collective-permute-start.34 = (f32[1,66,1024]{2,1,0:T(8,128)S(1)}, f32[1,66,1024]{2,1,0:T(8,128)S(1)}, u32[]{:S(2)}, u32[]{:S(2)}) collective-permute-start(f32[1,66,1024]{2,1,0:T(8,128)S(1)} %get-tuple-element.11), channel_id=1, source_target_pairs={{1,0},{2,1},{3,2},{4,3},{5,4},{6,5},{7,6},{8,7},{9,8},{10,9},{11,1... | collective-permute-start | bytes 811016 | tf_op jit(solution)/shard_map/ppermute | solution.py:23
  (36 other events, 1304.1 us)
Sparse Core Ops, SparseCore 0:
  55.2 52.8 all-gather.4
  348.5 81.5 reduce-scatter.2
  433.0 55.4 all-gather.6
  685.4 82.6 reduce-scatter.4
where the time goes:
time: 786 us; the launch traced here: 775 us
  other arithmetic  276 us (35%)
  waiting for transfers between devices  199 us (25%)
  local copies, waits for them, and re-layouts  132 us (17%)
  starting transfers between devices  106 us (13%)
  blocking collectives  46.6 us (6%)
  between operations  15.2 us (2%)
    scatter-add x2, other arithmetic, on_device(): source = jnp.zeros((nblocks, 128), jnp.float32).at[target].add(jnp.where(...  118 us
    reduce_scatter x2, waiting for transfers between devices, on_device(): iface = lax.psum_scatter(values, 'tool', scatter_dimension=0, tiled=True)  99.7 us
    gather x2, local copies, waits for them, and re-layouts, on_device(): force = bead_gain * sigma.reshape(-1)[bead_ids]  63.6 us
    gather x2, local copies, waits for them, and re-layouts, on_device(): values = jnp.where(mine[:, None], field_blocks[target], 0.0)  55.3 us
    ppermute x18, starting transfers between devices, with_halo(): lax.ppermute(lax.slice_in_dim(block, block.shape[dim] - width, None, axis...  55.1 us
    ppermute x18, starting transfers between devices, with_halo(): lax.ppermute(lax.slice_in_dim(block, 0, width, axis=dim), axis, backward)  51.2 us
    add x8, other arithmetic, on_device(): field = field + diffuse_step * total + source_step * source  50.4 us
    ppermute x18, waiting for transfers between devices, with_halo(): lax.ppermute(lax.slice_in_dim(block, 0, width, axis=dim), axis, backward)  47 us
  transfers between devices with their start and end apart: 40, of which 26 were waited for; matrix products, arithmetic and copies ran while one was open for 11% of the time, Pallas kernels for 0%

commit v1 on v0

v1 whole, which is shorter than its diff:
```python
import functools

import jax
import jax.numpy as jnp
from jax import lax
from jax.experimental import pallas as pl
from jax.experimental.pallas import tpu as pltpu
from jax.sharding import PartitionSpec as P

STEPS = 2
SWEEPS = 4
CAP = 64
LANES = 128
TILE = 8
NZ = 2

diffuse_step = 0.12
source_step = 0.25
shell_step = 0.5
face_step = 0.5 * diffuse_step


def split_pair(x):
    hi = x.astype(jnp.bfloat16)
    lo = (x - hi.astype(jnp.float32)).astype(jnp.bfloat16)
    return hi, lo


def one_hot(mask):
    return jnp.where(mask, 1.0, 0.0).astype(jnp.bfloat16)


def fold_rows(acc):
    for shift in (4, 2, 1):
        acc = acc + pltpu.roll(acc, shift, 0)
    return acc


def column_of(row):
    return jnp.transpose(jnp.broadcast_to(row, (LANES, LANES)))


def kernel(
    dims,
    tool_hbm,
    mat_hbm,
    cond,
    theta0,
    base_rate,
    film,
    contact,
    slab_rows,
    block_rows,
    bead_rows,
    gain_rows,
    tool_out,
    shell_out,
    contact_out,
    F,
    K,
    mat,
    Gx,
    Gy,
    Gz,
    SRC,
    W,
    FG,
    O,
    PM,
    PT,
    XB,
    R,
    A,
    BT,
    acc,
    slot_col,
    lin_col,
    metas,
    metar,
    gidx_v,
    gidx_s,
    ys,
    yr,
    kys,
    kyr,
    msg1s,
    msg1r,
    msg2s,
    msg2r,
    backs,
    backr,
    theta1,
    load_sem,
    out_sem,
    idx_sem,
    xss,
    xrs,
    yss,
    yrs,
    kss,
    krs,
    metass,
    metars,
    m1ss,
    m1rs,
    m2ss,
    m2rs,
    bss,
    brs,
):
    n_tool, n_blank, SX, SY, ZB, BLK, BEADROWS = dims
    slots = n_tool * CAP
    voxel_blocks = SX * SY * ZB
    YT = SY // TILE
    NC = ZB // NZ
    groups = BLK // LANES
    qgroups = slots // LANES
    t = lax.axis_index("tool")
    b = lax.axis_index("blank")
    has_left, has_right = t > 0, t < n_tool - 1
    has_down, has_up = b > 0, b < n_blank - 1

    loads = []
    for zb in range(ZB):
        loads.append(
            pltpu.make_async_copy(
                mat_hbm.at[:, :, pl.ds(zb * LANES, LANES)],
                mat.at[:, zb],
                load_sem.at[1, zb],
            )
        )
    for zb in range(ZB):
        loads.append(
            pltpu.make_async_copy(
                tool_hbm.at[:, :, pl.ds(zb * LANES, LANES)],
                F.at[0, pl.ds(1, SX), 1 + zb, pl.ds(TILE, SY), :],
                load_sem.at[0, zb],
            )
        )
    for copy in loads:
        copy.start()

    barrier = pltpu.get_barrier_semaphore()

    @pl.loop(1, n_tool)
    def _(off):
        pl.semaphore_signal(
            barrier, inc=1, device_id={"tool": lax.rem(t + off, n_tool)}, device_id_type=MESH
        )

    @pl.when(has_down)
    def _():
        pl.semaphore_signal(barrier, inc=1, device_id={"blank": b - 1}, device_id_type=MESH)

    @pl.when(has_up)
    def _():
        pl.semaphore_signal(barrier, inc=1, device_id={"blank": b + 1}, device_id_type=MESH)

    def clear_plane(plane):
        @pl.loop(0, ZB)
        def _(zb):
            zeros = jnp.zeros((SY, LANES), jnp.float32)
            K[plane, zb, pl.ds(TILE, SY), :] = zeros
            F[0, plane, 1 + zb, pl.ds(TILE, SY), :] = zeros
            F[1, plane, 1 + zb, pl.ds(TILE, SY), :] = zeros

    @pl.when(jnp.logical_not(has_left))
    def _():
        clear_plane(0)

    @pl.when(jnp.logical_not(has_right))
    def _():
        clear_plane(SX + 1)

    def clear_rim(side):
        zeros = jnp.zeros((ZB, SX, LANES), jnp.float32)
        yr[0, side] = zeros
        yr[1, side] = zeros
        kyr[side] = zeros

    @pl.when(jnp.logical_not(has_down))
    def _():
        clear_rim(0)

    @pl.when(jnp.logical_not(has_up))
    def _():
        clear_rim(1)

    @pl.loop(1, SX + 1)
    def _(p):
        zeros = jnp.zeros((SY, LANES), jnp.float32)
        for par in range(2):
            F[par, p, 0, pl.ds(TILE, SY), :] = zeros
            F[par, p, ZB + 1, pl.ds(TILE, SY), :] = zeros

    sub8 = lax.broadcasted_iota(jnp.int32, (TILE, LANES), 0)
    lane8 = lax.broadcasted_iota(jnp.int32, (TILE, LANES), 1)

    def row8(ref, g):
        return jnp.broadcast_to(ref[pl.ds(g, 1), :], (TILE, LANES))

    for g in range(groups):
        slot_col[pl.ds(g * LANES, LANES), :] = column_of(slab_rows[pl.ds(g, 1), :])
        blk = block_rows[pl.ds(g, 1), :]
        yl = (blk // ZB) % SY
        lin = ((blk // (ZB * SY)) * ZB + blk % ZB) * SY + yl
        lin_col[pl.ds(g * LANES, LANES), :] = column_of(lin)

    slot_rows = []
    for g in range(groups):
        mine = row8(slab_rows, g)

        def count(i, total, mine=mine, g=g):
            other = slot_col[pl.ds(pl.multiple_of(i * TILE, TILE), TILE), :]
            before = (sub8 + i * TILE) < (lane8 + g * LANES)
            return total + jnp.where((other == mine) & before, 1, 0)

        rank = fold_rows(
            lax.fori_loop(0, (g + 1) * LANES // TILE, count, jnp.zeros((TILE, LANES), jnp.int32))
        )
        slot_rows.append(mine * CAP + rank)
    for g in range(groups):
        slot_col[pl.ds(g * LANES, LANES), :] = column_of(slot_rows[g][0:1])

    @pl.loop(0, slots // LANES)
    def _(i):
        rows = lax.broadcasted_iota(jnp.int32, (LANES, LANES), 0) + i * LANES
        for g in range(groups):
            PM[pl.ds(pl.multiple_of(i * LANES, LANES), LANES), g * LANES : (g + 1) * LANES] = one_hot(
                rows == jnp.broadcast_to(slot_rows[g][0:1], (LANES, LANES))
            )

    @pl.loop(0, qgroups)
    def _(q):
        def part(i, total):
            at = pl.ds(pl.multiple_of(i * 16, 16), 16)
            hit = slot_col[at, :] == (lax.broadcasted_iota(jnp.int32, (16, LANES), 1) + q * LANES)
            PT[at, pl.ds(pl.multiple_of(q * LANES, LANES), LANES)] = one_hot(hit)
            named = jnp.where(hit, lin_col[at, :] + 1, 0)
            return total + named[:TILE] + named[TILE:]

        total = lax.fori_loop(0, BLK // 16, part, jnp.zeros((TILE, LANES), jnp.int32), unroll=4)
        metas[q] = fold_rows(total) - 1

    pl.semaphore_wait(barrier, n_tool - 1 + jnp.where(has_down, 1, 0) + jnp.where(has_up, 1, 0))

    def partner(off):
        return lax.rem(t + off, n_tool)

    def source_of(off):
        return lax.rem(t + n_tool - off, n_tool)

    def meta_copy(d, s):
        return pltpu.make_async_remote_copy(
            src_ref=metas.at[d // 2],
            dst_ref=metar.at[s],
            send_sem=metass.at[d],
            recv_sem=metars.at[s],
            device_id={"tool": d},
            device_id_type=MESH,
        )

    def row_copy(src, dst, ssem, rsem):
        def make(d, s):
            return pltpu.make_async_remote_copy(
                src_ref=src.at[d],
                dst_ref=dst.at[s],
                send_sem=ssem.at[d],
                recv_sem=rsem.at[s],
                device_id={"tool": d},
                device_id_type=MESH,
            )

        return make

    msg1_copy = row_copy(msg1s, msg1r, m1ss, m1rs)
    msg2_copy = row_copy(msg2s, msg2r, m2ss, m2rs)
    back_copy = [
        row_copy(backs.at[k], backr.at[k], bss.at[k], brs.at[k]) for k in range(STEPS)
    ]

    def send_all(make, first, last):
        @pl.loop(first, last)
        def _(off):
            make(partner(off), t).start()

    def wait_arrivals(make):
        @pl.loop(1, n_tool)
        def _(off):
            make(partner(off), source_of(off)).wait_recv()

    def wait_sends(make):
        @pl.loop(1, n_tool)
        def _(off):
            make(partner(off), t).wait_send()

    def x_copy(way, par, c):
        zs = pl.ds(1 + c * NZ, NZ)
        rows = pl.ds(TILE, SY)
        src, dst = (1, SX + 1) if way == 0 else (SX, 0)
        return pltpu.make_async_remote_copy(
            src_ref=F.at[par, src, zs, rows, :],
            dst_ref=F.at[par, dst, zs, rows, :],
            send_sem=xss.at[par, way, c],
            recv_sem=xrs.at[par, way, c],
            device_id={"tool": jnp.where(has_left, t - 1, t + 1) if way == 0 else jnp.where(has_right, t + 1, t - 1)},
            device_id_type=MESH,
        )

    def y_copy(way, par, c):
        zs = pl.ds(c * NZ, NZ)
        return pltpu.make_async_remote_copy(
            src_ref=ys.at[par, way, zs],
            dst_ref=yr.at[par, 1 - way, zs],
            send_sem=yss.at[par, way, c],
            recv_sem=yrs.at[par, way, c],
            device_id={"blank": jnp.where(has_down, b - 1, b + 1) if way == 0 else jnp.where(has_up, b + 1, b - 1)},
            device_id_type=MESH,
        )

    def kx_copy(way):
        rows = pl.ds(TILE, SY)
        src, dst = (1, SX + 1) if way == 0 else (SX, 0)
        return pltpu.make_async_remote_copy(
            src_ref=K.at[src, :, rows, :],
            dst_ref=K.at[dst, :, rows, :],
            send_sem=kss.at[0, way],
            recv_sem=krs.at[0, way],
            device_id={"tool": jnp.where(has_left, t - 1, t + 1) if way == 0 else jnp.where(has_right, t + 1, t - 1)},
            device_id_type=MESH,
        )

    def ky_copy(way):
        return pltpu.make_async_remote_copy(
            src_ref=kys.at[way],
            dst_ref=kyr.at[1 - way],
            send_sem=kss.at[1, way],
            recv_sem=krs.at[1, way],
            device_id={"blank": jnp.where(has_down, b - 1, b + 1) if way == 0 else jnp.where(has_up, b + 1, b - 1)},
            device_id_type=MESH,
        )

    sends_x, sends_y = (has_left, has_right), (has_down, has_up)
    gets_x, gets_y = (has_right, has_left), (has_up, has_down)

    def at_each(flags, act):
        for way in range(2):
            @pl.when(flags[way])
            def _(way=way):
                act(way)

    for zb in range(ZB):
        loads[zb].wait()

    @pl.loop(0, SX)
    def _(xl):
        @pl.loop(0, ZB)
        def _(zb):
            m = mat[xl, zb]
            low, mid, top = (m & 1) != 0, (m & 2) != 0, (m & 4) != 0
            pairs = [jnp.where(low, cond[2 * i + 1], cond[2 * i]) for i in range(4)]
            quads = [jnp.where(mid, pairs[2 * i + 1], pairs[2 * i]) for i in range(2)]
            K[1 + xl, zb, pl.ds(TILE, SY), :] = jnp.where(top, quads[1], quads[0])

    at_each(sends_x, lambda way: kx_copy(way).start())

    @pl.loop(0, ZB)
    def _(zb):
        for xl in range(SX):
            kys[0, zb, pl.ds(xl, 1), :] = K[1 + xl, zb, pl.ds(TILE, 1), :]
            kys[1, zb, pl.ds(xl, 1), :] = K[1 + xl, zb, pl.ds(TILE + SY - 1, 1), :]

    at_each(sends_y, lambda way: ky_copy(way).start())

    outflow = film[...] * (theta0[...] - contact[...])
    hi, lo = split_pair(outflow)
    XB[:, 0:LANES] = hi
    XB[:, LANES : 2 * LANES] = lo
    part_rows = min(512, slots)
    step_rows = min(512, voxel_blocks)

    def pack(write, columns):
        @pl.loop(0, slots // part_rows)
        def _(i):
            got = jnp.dot(
                PM[pl.ds(pl.multiple_of(i * part_rows, part_rows), part_rows), :],
                XB[:, columns : columns + 2 * LANES],
                preferred_element_type=jnp.float32,
            )
            rows = got[:, :LANES] + got[:, LANES:]
            write(i * (part_rows // CAP), rows.reshape(part_rows // CAP, CAP, LANES))

    def write1(d, rows):
        msg1s[pl.ds(d, part_rows // CAP)] = rows

    pack(write1, 0)
    send_all(meta_copy, 1, n_tool)
    send_all(msg1_copy, 1, n_tool)
    metar[t] = metas[t // 2]
    msg1r[t] = msg1s[t]

    def pack_y(par, c):
        for i in range(NZ):
            for xl in range(SX):
                zb = c * NZ + i
                ys[par, 0, zb, pl.ds(xl, 1), :] = F[par, 1 + xl, 1 + zb, pl.ds(TILE, 1), :]
                ys[par, 1, zb, pl.ds(xl, 1), :] = F[par, 1 + xl, 1 + zb, pl.ds(TILE + SY - 1, 1), :]

    def unpack_y(par, c):
        for i in range(NZ):
            for xl in range(SX):
                zb = c * NZ + i
                F[par, 1 + xl, 1 + zb, pl.ds(TILE - 1, 1), :] = yr[par, 0, zb, pl.ds(xl, 1), :]
                F[par, 1 + xl, 1 + zb, pl.ds(TILE + SY, 1), :] = yr[par, 1, zb, pl.ds(xl, 1), :]

    for zb in range(ZB):
        loads[ZB + zb].wait()

    @pl.loop(0, NC)
    def _(c):
        at_each(sends_x, lambda way: x_copy(way, 0, c).start())
        pack_y(0, c)
        at_each(sends_y, lambda way: y_copy(way, 0, c).start())

    for j in range(BEADROWS // TILE):
        @pl.loop(0, TILE)
        def _(i, j=j):
            at = pl.ds(pl.multiple_of(i * LANES, LANES), LANES)
            shell = bead_rows[pl.ds(j * TILE + i, 1), :]
            row, lane = shell // LANES, shell % LANES
            A[:, at] = one_hot(
                lax.broadcasted_iota(jnp.int32, (BLK, LANES), 0) == jnp.broadcast_to(row, (BLK, LANES))
            )
            here = lax.broadcasted_iota(jnp.int32, (LANES, LANES), 0) == jnp.broadcast_to(lane, (LANES, LANES))
            held = jnp.where(here, jnp.broadcast_to(gain_rows[pl.ds(j * TILE + i, 1), :], (LANES, LANES)), 0.0)
            hi, lo = split_pair(held)
            BT[0:LANES, at] = hi
            BT[LANES : 2 * LANES, at] = lo

        part = lax.dot_general(
            A[...], BT[...], (((1,), (1,)), ((), ())), preferred_element_type=jnp.float32
        )
        if j == 0:
            acc[...] = part
        else:
            acc[...] += part

    sigma = 1.0 - 0.4 * jnp.tanh(theta0[...])
    rate = base_rate[...] + sigma * (acc[:, :LANES] + acc[:, LANES:])
    after = theta0[...] + shell_step * (sigma * rate - outflow)
    theta1[...] = after
    hi, lo = split_pair(film[...])
    XB[:, 0:LANES] = hi
    XB[:, LANES : 2 * LANES] = lo
    hi, lo = split_pair(film[...] * after)
    XB[:, 2 * LANES : 3 * LANES] = hi
    XB[:, 3 * LANES : 4 * LANES] = lo

    def write2(d, rows, first):
        msg2s[pl.ds(d, part_rows // CAP), first : first + CAP, :] = rows

    pack(lambda d, rows: write2(d, rows, 0), 0)
    pack(lambda d, rows: write2(d, rows, CAP), 2 * LANES)
    msg2r[t] = msg2s[t]

    lane = lax.broadcasted_iota(jnp.int32, (SY, LANES), 1)
    last_lane, first_lane = lane == LANES - 1, lane == 0

    @pl.loop(0, SX)
    def _(xl):
        here = K[1 + xl, 0, pl.ds(TILE, SY), :]
        turned = pltpu.roll(here, LANES - 1, 1)
        Gz[xl, 0] = face_step * turned
        for zb in range(ZB):
            if zb < ZB - 1:
                after_here = K[1 + xl, zb + 1, pl.ds(TILE, SY), :]
                turned_after = pltpu.roll(after_here, LANES - 1, 1)
                up = jnp.where(last_lane, turned_after, turned)
            else:
                after_here, turned_after = here, turned
                up = jnp.where(last_lane, 0.0, turned)
            Gz[xl, 1 + zb] = face_step * (here + up)
            here, turned = after_here, turned_after

    def x_faces(p):
        @pl.loop(0, ZB)
        def _(zb):
            Gx[p, zb] = face_step * (K[p, zb, pl.ds(TILE, SY), :] + K[p + 1, zb, pl.ds(TILE, SY), :])

    @pl.loop(1, SX)
    def _(p):
        x_faces(p)

    wait_arrivals(meta_copy)
    even = lax.rem(t, 2) == 0
    lin_rows = []
    for q in range(qgroups):
        first, second = metar[2 * q], metar[2 * q + 1]
        first = jnp.where(even, first, pltpu.roll(first, CAP, 1))
        second = jnp.where(even, pltpu.roll(second, CAP, 1), second)
        lin = jnp.where(lane8 < CAP, first, second)
        lin_rows.append(lin)
        gidx_v[pl.ds(q, 1), :] = jnp.maximum(lin[0:1], 0)
    to_smem = pltpu.make_async_copy(gidx_v, gidx_s, idx_sem)
    to_smem.start()

    @pl.loop(0, voxel_blocks // LANES)
    def _(i):
        rows = lax.broadcasted_iota(jnp.int32, (LANES, LANES), 0) + i * LANES
        for q in range(qgroups):
            O[pl.ds(pl.multiple_of(i * LANES, LANES), LANES), q * LANES : (q + 1) * LANES] = one_hot(
                rows == jnp.broadcast_to(lin_rows[q][0:1], (LANES, LANES))
            )

    to_smem.wait()

    at_each(gets_y, lambda way: ky_copy(way).wait_recv())

    @pl.loop(0, ZB)
    def _(zb):
        for xl in range(SX):
            K[1 + xl, zb, pl.ds(TILE - 1, 1), :] = kyr[0, zb, pl.ds(xl, 1), :]
            K[1 + xl, zb, pl.ds(TILE + SY, 1), :] = kyr[1, zb, pl.ds(xl, 1), :]

    @pl.loop(0, SX)
    def _(xl):
        @pl.loop(0, ZB)
        def _(zb):
            Gy[xl, zb, pl.ds(TILE - 1, 1), :] = face_step * (
                K[1 + xl, zb, pl.ds(TILE - 1, 1), :] + K[1 + xl, zb, pl.ds(TILE, 1), :]
            )
            Gy[xl, zb, pl.ds(TILE, SY), :] = face_step * (
                K[1 + xl, zb, pl.ds(TILE, SY), :] + K[1 + xl, zb, pl.ds(TILE + 1, SY), :]
            )

    at_each(gets_x, lambda way: kx_copy(way).wait_recv())
    x_faces(0)
    x_faces(SX)

    def split_rows(src, rows, first, column):
        @pl.loop(0, n_tool)
        def _(s):
            hi, lo = split_pair(src[s, first : first + rows, :])
            at = pl.ds(pl.multiple_of(s * CAP, CAP), CAP)
            R[at, column : column + LANES] = hi
            R[at, column + LANES : column + 2 * LANES] = lo

    def scatter(column, write):
        @pl.loop(0, voxel_blocks // step_rows)
        def _(m):
            at = pl.ds(pl.multiple_of(m * step_rows, step_rows), step_rows)
            got = jnp.dot(
                O[at, :], R[:, column : column + 2 * LANES], preferred_element_type=jnp.float32
            )
            write(at, source_step * (got[:, :LANES] + got[:, LANES:]))

    def to_source(at, rows):
        SRC[at, :] = rows

    def to_weight(at, rows):
        W[at, :] = rows

    wait_arrivals(msg1_copy)
    split_rows(msg1r, CAP, 0, 0)
    scatter(0, to_source)

    lane_t = lax.broadcasted_iota(jnp.int32, (TILE, LANES), 1)
    top_lane, low_lane = lane_t == LANES - 1, lane_t == 0

    def planes(cur, c, yt, first, last):
        new = 1 - cur
        y0 = pl.multiple_of(yt * TILE, TILE)
        rows = pl.ds(pl.multiple_of(y0 + TILE, TILE), TILE)

        def temp(p, i, shift=0):
            if shift:
                return F[cur, p, 1 + c * NZ + i, pl.ds(y0 + TILE + shift, TILE), :]
            return F[cur, p, 1 + c * NZ + i, rows, :]

        def face_x(p, i):
            return Gx[p, c * NZ + i, pl.ds(y0, TILE), :]

        center = [temp(first, i) for i in range(NZ)]
        below = [face_x(first - 1, i) * (center[i] - temp(first - 1, i)) for i in range(NZ)]
        for p in range(first, last):
            xl = p - 1
            ahead = [temp(p + 1, i) for i in range(NZ)]
            above = [face_x(p, i) * (ahead[i] - center[i]) for i in range(NZ)]
            line = [temp(p, -1)] + center + [temp(p, NZ)]
            turned = [None] + [pltpu.roll(line[i], LANES - 1, 1) for i in range(1, NZ + 2)]
            flow = [Gz[xl, c * NZ, pl.ds(y0, TILE), :] * (turned[1] - line[0])]
            for i in range(1, NZ + 1):
                up = jnp.where(top_lane, turned[i + 1], turned[i])
                flow.append(Gz[xl, c * NZ + i, pl.ds(y0, TILE), :] * (up - line[i]))
            moved = [pltpu.roll(flow[i], 1, 1) for i in range(NZ + 1)]
            for i in range(NZ):
                z_part = flow[i + 1] - jnp.where(low_lane, moved[i], moved[i + 1])
                y_high = Gy[xl, c * NZ + i, rows, :] * (temp(p, i, 1) - center[i])
                y_low = Gy[xl, c * NZ + i, pl.ds(y0 + TILE - 1, TILE), :] * (center[i] - temp(p, i, -1))
                at = pl.multiple_of((xl * ZB + c * NZ + i) * SY + y0, TILE)
                total = (above[i] - below[i]) + (y_high - y_low) + z_part
                F[new, p, 1 + c * NZ + i, rows, :] = center[i] + (total + SRC[pl.ds(at, TILE), :])
            center, below = ahead, above

    def keep(cur, with_source):
        @pl.loop(0, SX)
        def _(xl):
            @pl.loop(0, ZB)
            def _(zb):
                at = pl.ds(pl.multiple_of((xl * ZB + zb) * SY, SY), SY)
                now = F[cur, 1 + xl, 1 + zb, pl.ds(TILE, SY), :]
                FG[at, :] = now
                if with_source:
                    SRC[at, :] = SRC[at, :] - W[at, :] * now

    def collect(k):
        @pl.loop(0, n_tool)
        def _(s):
            q = s // 2
            lane0 = lax.rem(s, 2) * CAP

            @pl.loop(0, CAP // TILE)
            def _(j):
                for i in range(TILE):
                    row = gidx_s[q, lane0 + j * TILE + i]
                    backs[k, s, pl.ds(pl.multiple_of(j * TILE, TILE) + i, 1), :] = FG[pl.ds(row, 1), :]

    total_sweeps = STEPS * SWEEPS

    @pl.loop(0, total_sweeps)
    def _(s):
        cur = lax.rem(s, 2)
        new = 1 - cur

        @pl.loop(0, NC)
        def _(c):
            at_each(gets_y, lambda way: y_copy(way, cur, c).wait_recv())
            unpack_y(cur, c)
            at_each(gets_x, lambda way: x_copy(way, cur, c).wait_recv())

            @pl.when(s >= 1)
            def _():
                at_each(sends_x, lambda way: x_copy(way, new, c).wait_send())
                at_each(sends_y, lambda way: y_copy(way, new, c).wait_send())

            @pl.loop(0, YT)
            def _(yt):
                planes(cur, c, yt, 1, 2)
                planes(cur, c, yt, SX, SX + 1)

            @pl.when(s < total_sweeps - 1)
            def _():
                at_each(sends_x, lambda way: x_copy(way, new, c).start())

            @pl.loop(0, YT)
            def _(yt):
                planes(cur, c, yt, 2, SX)

            @pl.when(s < total_sweeps - 1)
            def _():
                pack_y(new, c)
                at_each(sends_y, lambda way: y_copy(way, new, c).start())

        half = (n_tool + 1) // 2

        @pl.when(s == 0)
        def _():
            send_all(msg2_copy, 1, half)

        @pl.when(s == 1)
        def _():
            send_all(msg2_copy, half, n_tool)

        @pl.when(s == 2)
        def _():
            wait_arrivals(msg2_copy)
            split_rows(msg2r, CAP, 0, 0)
            split_rows(msg2r, CAP, CAP, 2 * LANES)
            scatter(0, to_weight)

        @pl.when(s == SWEEPS - 1)
        def _():
            scatter(2 * LANES, to_source)
            keep(new, True)

        @pl.when(s == SWEEPS)
        def _():
            collect(0)
            send_all(back_copy[0], 1, half)

        @pl.when(s == SWEEPS + 1)
        def _():
            send_all(back_copy[0], half, n_tool)

    keep(0, False)
    stores = [
        pltpu.make_async_copy(
            FG.at[pl.ds((xl * ZB + zb) * SY, SY), :],
            tool_out.at[xl, :, pl.ds(zb * LANES, LANES)],
            out_sem.at[xl, zb],
        )
        for xl in range(SX)
        for zb in range(ZB)
    ]
    collect(1)
    send_all(back_copy[1], 1, n_tool)
    for copy in stores:
        copy.start()

    def contact_of(k):
        backr[k, t] = backs[k, t]
        wait_arrivals(back_copy[k])
        split_rows(backr.at[k], CAP, 0, 0)
        got = jnp.dot(PT[...], R[:, 0 : 2 * LANES], preferred_element_type=jnp.float32)
        return got[:, :LANES] + got[:, LANES:]

    flux = film[...] * (contact_of(0) - theta1[...])
    sigma = 1.0 - 0.4 * jnp.tanh(theta1[...])
    rate = base_rate[...] + sigma * (acc[:, :LANES] + acc[:, LANES:])
    shell_out[...] = theta1[...] + shell_step * (flux + sigma * rate)
    contact_out[...] = contact_of(1)

    wait_sends(meta_copy)
    wait_sends(msg1_copy)
    wait_sends(msg2_copy)
    wait_sends(back_copy[0])
    wait_sends(back_copy[1])
    at_each(sends_x, lambda way: kx_copy(way).wait_send())
    at_each(sends_y, lambda way: ky_copy(way).wait_send())

    last = (total_sweeps - 1) % 2

    @pl.loop(0, NC)
    def _(c):
        at_each(sends_x, lambda way: x_copy(way, last, c).wait_send())
        at_each(sends_y, lambda way: y_copy(way, last, c).wait_send())

    for copy in stores:
        copy.wait()


MESH = pl.DeviceIdType.MESH


def on_device(n_tool, n_blank, tool_temp, material, conductivity, shell_temp, base_rate, film, contact_temp, pair_slab, pair_block, bead_ids, bead_gain):
    SX, SY, SZ = tool_temp.shape
    ZB = SZ // LANES
    NC = ZB // NZ
    BLK = shell_temp.shape[0]
    beadrows = bead_ids.shape[0] // LANES
    slots = n_tool * CAP
    voxel_blocks = SX * SY * ZB
    f32, bf16, i32 = jnp.float32, jnp.bfloat16, jnp.int32
    V = pltpu.VMEM
    dma = pltpu.SemaphoreType.DMA
    scratch = [
        V((2, SX + 2, ZB + 2, SY + 2 * TILE, LANES), f32),
        V((SX + 2, ZB, SY + 2 * TILE, LANES), f32),
        V((SX, ZB, SY, LANES), i32),
        V((SX + 1, ZB, SY, LANES), f32),
        V((SX, ZB, SY + TILE, LANES), f32),
        V((SX, ZB + 1, SY, LANES), f32),
        V((voxel_blocks, LANES), f32),
        V((voxel_blocks, LANES), f32),
        V((voxel_blocks, LANES), f32),
        V((voxel_blocks, slots), bf16),
        V((slots, BLK), bf16),
        V((BLK, slots), bf16),
        V((BLK, 4 * LANES), bf16),
        V((slots, 4 * LANES), bf16),
        V((BLK, TILE * LANES), bf16),
        V((2 * LANES, TILE * LANES), bf16),
        V((BLK, 2 * LANES), f32),
        V((BLK, LANES), i32),
        V((BLK, LANES), i32),
        V((slots // LANES, TILE, LANES), i32),
        V((n_tool, TILE, LANES), i32),
        V((slots // LANES, LANES), i32),
        pltpu.SMEM((slots // LANES, LANES), i32),
        V((2, 2, ZB, SX, LANES), f32),
        V((2, 2, ZB, SX, LANES), f32),
        V((2, ZB, SX, LANES), f32),
        V((2, ZB, SX, LANES), f32),
        V((n_tool, CAP, LANES), f32),
        V((n_tool, CAP, LANES), f32),
        V((n_tool, 2 * CAP, LANES), f32),
        V((n_tool, 2 * CAP, LANES), f32),
        V((STEPS, n_tool, CAP, LANES), f32),
        V((STEPS, n_tool, CAP, LANES), f32),
        V((BLK, LANES), f32),
        dma((2, ZB)),
        dma((SX, ZB)),
        dma,
        dma((2, 2, NC)),
        dma((2, 2, NC)),
        dma((2, 2, NC)),
        dma((2, 2, NC)),
        dma((2, 2)),
        dma((2, 2)),
        dma((n_tool,)),
        dma((n_tool,)),
        dma((n_tool,)),
        dma((n_tool,)),
        dma((n_tool,)),
        dma((n_tool,)),
        dma((STEPS, n_tool)),
        dma((STEPS, n_tool)),
    ]
    whole = pl.BlockSpec(memory_space=pltpu.VMEM)
    far = pl.BlockSpec(memory_space=pl.ANY)
    return pl.pallas_call(
        functools.partial(kernel, (n_tool, n_blank, SX, SY, ZB, BLK, beadrows)),
        out_shape=(
            jax.ShapeDtypeStruct(tool_temp.shape, f32),
            jax.ShapeDtypeStruct(shell_temp.shape, f32),
            jax.ShapeDtypeStruct(shell_temp.shape, f32),
        ),
        in_specs=[far, far, pl.BlockSpec(memory_space=pltpu.SMEM)] + [whole] * 8,
        out_specs=(far, whole, whole),
        scratch_shapes=scratch,
        compiler_params=pltpu.CompilerParams(
            collective_id=0, has_side_effects=True, vmem_limit_bytes=60 * 2**20
        ),
    )(
        tool_temp,
        material,
        conductivity,
        shell_temp,
        base_rate,
        film,
        contact_temp,
        pair_slab.reshape(BLK // LANES, LANES),
        pair_block.reshape(BLK // LANES, LANES),
        bead_ids.reshape(beadrows, LANES),
        bead_gain.reshape(beadrows, LANES),
    )


def solution(mesh):
    placed = (
        P("tool", "blank", None),
        P("tool", "blank", None),
        P(),
        P(("blank", "tool"), None),
        P(("blank", "tool"), None),
        P(("blank", "tool"), None),
        P(("blank", "tool"), None),
        P(("blank", "tool"), None),
        P(("blank", "tool")),
        P(("blank", "tool")),
        P(("blank", "tool")),
    )
    return jax.shard_map(
        functools.partial(on_device, mesh.shape["tool"], mesh.shape["blank"]),
        mesh=mesh,
        in_specs=placed,
        out_specs=(
            P("tool", "blank", None),
            P(("blank", "tool"), None),
            P(("blank", "tool"), None),
        ),
        check_vma=False,
    )
```

time: 786 us -> 367 us (0.47); the launches traced: 775 us -> 367 us
  Pallas kernels: 0 us -> 361 us
  other arithmetic: 276 us -> 0 us
  waiting for transfers between devices: 199 us -> 0 us
  local copies, waits for them, and re-layouts: 132 us -> 4.63 us
  starting transfers between devices: 106 us -> 0 us
  blocking collectives: 46.6 us -> 0 us
  between operations: 15.2 us -> 0.66 us
    pallas_call x0 -> x1, Pallas kernels: none -> 361 us  [on_device(): pl.pallas_call(functools.partial(kernel, (n_tool, n_blank, SX, SY, ZB, BL...]
    scatter-add x4 -> x0, other arithmetic: 162 us -> none  [the longest x2 118 us: on_device(): source = jnp.zeros((nblocks, 128), jnp.float32).at[target].add(jnp.where(...]
    gather x4 -> x0, local copies, waits for them, and re-layouts: 119 us -> none  [the longest x2 63.6 us: on_device(): force = bead_gain * sigma.reshape(-1)[bead_ids]]
    ppermute x36 -> x0, starting transfers between devices: 106 us -> none  [the longest x18 55.1 us: with_halo(): lax.ppermute(lax.slice_in_dim(block, block.shape[dim] - width, None, axis...]
    reduce_scatter x2 -> x0, waiting for transfers between devices: 99.7 us -> none  [on_device(): iface = lax.psum_scatter(values, 'tool', scatter_dimension=0, tiled=True)]
    ppermute x36 -> x0, waiting for transfers between devices: 69.6 us -> none  [the longest x18 47 us: with_halo(): lax.ppermute(lax.slice_in_dim(block, 0, width, axis=dim), axis, backward)]
    add x9 -> x0, other arithmetic: 52.3 us -> none  [the longest x8 50.4 us: on_device(): field = field + diffuse_step * total + source_step * source]
    all_gather x2 -> x0, blocking collectives: 46.6 us -> none  [the longest x1 23.8 us: on_device(): lax.all_gather(slab, 'tool', axis=0, tiled=True)]
  transfers between devices with their start and end apart: 40 -> 0, of which waited for: 26 -> 0; matrix products, arithmetic and copies ran while one was open for 11% -> 0% of each run, Pallas kernels for 0% -> 0%
where the time goes in v1:
time: 367 us
  Pallas kernels  361 us (98%)
  local copies, waits for them, and re-layouts  4.63 us (1%)
    pallas_call x1, Pallas kernels, on_device(): pl.pallas_call(functools.partial(kernel, (n_tool, n_blank, SX, SY, ZB, BL...  361 us

profile of v1, /device:TPU:96, one launch (start us, length us, event | category | flops | bytes accessed | tf_op | source)
XLA Modules:
  0.0 366.7 jit_solution(2822023246474290091)
XLA Ops:
  0.6 361.4 %shard_map.130 = (f32[8,64,1024]{2,1,0:T(8,128)}, f32[512,128]{1,0:T(8,128)}, f32[512,128]{1,0:T(8,128)}) custom-call(f32[8,64,1024]{2,1,0:T(8,128)} %tool_hbm.1, s32[8,64,1024]{2,1,0:T(8,128)} %mat_hbm.1, f32[8]{0:T(128)} %cond.1, f32[512,128]{1,0:T(8,128)} %theta0.1, f32[512,128]{1,0:T(8,128)} %base_rate.1, f32[512,128]{1,0:T(8,128)} %film.1, ...), custom_call_target="tpu_custom_call" | custom-call | tf_op jit(solution)/shard_map/pallas_call | solution.py:811
  362.1 0.0 copy-start.1
  362.1 0.0 copy-start
  362.1 3.2 copy.17
  365.3 0.0 copy-done.1
  365.3 0.7 copy.18
  366.0 0.0 copy-done
  366.0 0.7 copy.19
Async XLA Ops:
  362.1 3.2 copy-start.1
  362.1 3.9 %copy-start = (f32[512,128]{1,0:T(8,128)S(1)}, f32[512,128]{1,0:T(8,128)}, u32[]{:S(2)}) copy-start(f32[512,128]{1,0:T(8,128)} %get-tuple-element.8) | copy-start | bytes 786436

commit v2 on v1

--- a/solution.py
+++ b/solution.py
@@ -12,7 +12,7 @@
 CAP = 64
 LANES = 128
 TILE = 8
-NZ = 2
+CHUNKS = 4
 
 diffuse_step = 0.12
 source_step = 0.25
@@ -56,12 +56,14 @@
     tool_out,
     shell_out,
     contact_out,
-    F,
+    FA,
+    FB,
     K,
     mat,
     Gx,
     Gy,
-    Gz,
+    GzH,
+    GzL,
     SRC,
     W,
     FG,
@@ -111,8 +113,9 @@
     n_tool, n_blank, SX, SY, ZB, BLK, BEADROWS = dims
     slots = n_tool * CAP
     voxel_blocks = SX * SY * ZB
-    YT = SY // TILE
-    NC = ZB // NZ
+    NC = CHUNKS
+    CY = SY // NC
+    F = (FA, FB)
     groups = BLK // LANES
     qgroups = slots // LANES
     t = lax.axis_index("tool")
@@ -133,7 +136,7 @@
         loads.append(
             pltpu.make_async_copy(
                 tool_hbm.at[:, :, pl.ds(zb * LANES, LANES)],
-                F.at[0, pl.ds(1, SX), 1 + zb, pl.ds(TILE, SY), :],
+                FA.at[pl.ds(1, SX), zb, pl.ds(TILE, SY), :],
                 load_sem.at[0, zb],
             )
         )
@@ -161,8 +164,8 @@
         def _(zb):
             zeros = jnp.zeros((SY, LANES), jnp.float32)
             K[plane, zb, pl.ds(TILE, SY), :] = zeros
-            F[0, plane, 1 + zb, pl.ds(TILE, SY), :] = zeros
-            F[1, plane, 1 + zb, pl.ds(TILE, SY), :] = zeros
+            FA[plane, zb, pl.ds(TILE, SY), :] = zeros
+            FB[plane, zb, pl.ds(TILE, SY), :] = zeros
 
     @pl.when(jnp.logical_not(has_left))
     def _():
@@ -185,13 +188,6 @@
     @pl.when(jnp.logical_not(has_up))
     def _():
         clear_rim(1)
-
-    @pl.loop(1, SX + 1)
-    def _(p):
-        zeros = jnp.zeros((SY, LANES), jnp.float32)
-        for par in range(2):
-            F[par, p, 0, pl.ds(TILE, SY), :] = zeros
-            F[par, p, ZB + 1, pl.ds(TILE, SY), :] = zeros
 
     sub8 = lax.broadcasted_iota(jnp.int32, (TILE, LANES), 0)
     lane8 = lax.broadcasted_iota(jnp.int32, (TILE, LANES), 1)
@@ -294,27 +290,30 @@
         def _(off):
             make(partner(off), t).wait_send()
 
+    left = {"tool": jnp.where(has_left, t - 1, t + 1)}
+    right = {"tool": jnp.where(has_right, t + 1, t - 1)}
+    down = {"blank": jnp.where(has_down, b - 1, b + 1)}
+    up = {"blank": jnp.where(has_up, b + 1, b - 1)}
+
     def x_copy(way, par, c):
-        zs = pl.ds(1 + c * NZ, NZ)
-        rows = pl.ds(TILE, SY)
+        rows = pl.ds(pl.multiple_of(TILE + c * CY, TILE), CY)
         src, dst = (1, SX + 1) if way == 0 else (SX, 0)
         return pltpu.make_async_remote_copy(
-            src_ref=F.at[par, src, zs, rows, :],
-            dst_ref=F.at[par, dst, zs, rows, :],
+            src_ref=F[par].at[src, :, rows, :],
+            dst_ref=F[par].at[dst, :, rows, :],
             send_sem=xss.at[par, way, c],
             recv_sem=xrs.at[par, way, c],
-            device_id={"tool": jnp.where(has_left, t - 1, t + 1) if way == 0 else jnp.where(has_right, t + 1, t - 1)},
+            device_id=left if way == 0 else right,
             device_id_type=MESH,
         )
 
-    def y_copy(way, par, c):
-        zs = pl.ds(c * NZ, NZ)
+    def y_copy(way, par):
         return pltpu.make_async_remote_copy(
-            src_ref=ys.at[par, way, zs],
-            dst_ref=yr.at[par, 1 - way, zs],
-            send_sem=yss.at[par, way, c],
-            recv_sem=yrs.at[par, way, c],
-            device_id={"blank": jnp.where(has_down, b - 1, b + 1) if way == 0 else jnp.where(has_up, b + 1, b - 1)},
+            src_ref=ys.at[par, way],
+            dst_ref=yr.at[par, 1 - way],
+            send_sem=yss.at[par, way],
+            recv_sem=yrs.at[par, way],
+            device_id=down if way == 0 else up,
             device_id_type=MESH,
         )
 
@@ -326,7 +325,7 @@
             dst_ref=K.at[dst, :, rows, :],
             send_sem=kss.at[0, way],
             recv_sem=krs.at[0, way],
-            device_id={"tool": jnp.where(has_left, t - 1, t + 1) if way == 0 else jnp.where(has_right, t + 1, t - 1)},
+            device_id=left if way == 0 else right,
             device_id_type=MESH,
         )
 
@@ -336,7 +335,7 @@
             dst_ref=kyr.at[1 - way],
             send_sem=kss.at[1, way],
             recv_sem=krs.at[1, way],
-            device_id={"blank": jnp.where(has_down, b - 1, b + 1) if way == 0 else jnp.where(has_up, b + 1, b - 1)},
+            device_id=down if way == 0 else up,
             device_id_type=MESH,
         )
 
@@ -399,19 +398,21 @@
     metar[t] = metas[t // 2]
     msg1r[t] = msg1s[t]
 
-    def pack_y(par, c):
-        for i in range(NZ):
+    def pack_y(par, way):
+        row = TILE if way == 0 else TILE + SY - 1
+
+        @pl.loop(0, ZB)
+        def _(zb):
             for xl in range(SX):
-                zb = c * NZ + i
-                ys[par, 0, zb, pl.ds(xl, 1), :] = F[par, 1 + xl, 1 + zb, pl.ds(TILE, 1), :]
-                ys[par, 1, zb, pl.ds(xl, 1), :] = F[par, 1 + xl, 1 + zb, pl.ds(TILE + SY - 1, 1), :]
-
-    def unpack_y(par, c):
-        for i in range(NZ):
+                ys[par, way, zb, pl.ds(xl, 1), :] = F[par][1 + xl, zb, pl.ds(row, 1), :]
+
+    def unpack_y(par, side):
+        row = TILE - 1 if side == 0 else TILE + SY
+
+        @pl.loop(0, ZB)
+        def _(zb):
             for xl in range(SX):
-                zb = c * NZ + i
-                F[par, 1 + xl, 1 + zb, pl.ds(TILE - 1, 1), :] = yr[par, 0, zb, pl.ds(xl, 1), :]
-                F[par, 1 + xl, 1 + zb, pl.ds(TILE + SY, 1), :] = yr[par, 1, zb, pl.ds(xl, 1), :]
+                F[par][1 + xl, zb, pl.ds(row, 1), :] = yr[par, side, zb, pl.ds(xl, 1), :]
 
     for zb in range(ZB):
         loads[ZB + zb].wait()
@@ -419,8 +420,10 @@
     @pl.loop(0, NC)
     def _(c):
         at_each(sends_x, lambda way: x_copy(way, 0, c).start())
-        pack_y(0, c)
-        at_each(sends_y, lambda way: y_copy(way, 0, c).start())
+
+    for way in range(2):
+        pack_y(0, way)
+    at_each(sends_y, lambda way: y_copy(way, 0).start())
 
     for j in range(BEADROWS // TILE):
         @pl.loop(0, TILE)
@@ -468,19 +471,14 @@
 
     @pl.loop(0, SX)
     def _(xl):
-        here = K[1 + xl, 0, pl.ds(TILE, SY), :]
-        turned = pltpu.roll(here, LANES - 1, 1)
-        Gz[xl, 0] = face_step * turned
+        line = [K[1 + xl, zb, pl.ds(TILE, SY), :] for zb in range(ZB)]
+        ahead = [pltpu.roll(k, LANES - 1, 1) for k in line] + [jnp.zeros((SY, LANES), jnp.float32)]
+        behind = [jnp.zeros((SY, LANES), jnp.float32)] + [pltpu.roll(k, 1, 1) for k in line]
         for zb in range(ZB):
-            if zb < ZB - 1:
-                after_here = K[1 + xl, zb + 1, pl.ds(TILE, SY), :]
-                turned_after = pltpu.roll(after_here, LANES - 1, 1)
-                up = jnp.where(last_lane, turned_after, turned)
-            else:
-                after_here, turned_after = here, turned
-                up = jnp.where(last_lane, 0.0, turned)
-            Gz[xl, 1 + zb] = face_step * (here + up)
-            here, turned = after_here, turned_after
+            high = jnp.where(last_lane, ahead[zb + 1], ahead[zb])
+            low = jnp.where(first_lane, behind[zb], behind[zb + 1])
+            GzH[xl, zb] = face_step * (line[zb] + high)
+            GzL[xl, zb] = face_step * (line[zb] + low)
 
     def x_faces(p):
         @pl.loop(0, ZB)
@@ -566,40 +564,34 @@
 
     lane_t = lax.broadcasted_iota(jnp.int32, (TILE, LANES), 1)
     top_lane, low_lane = lane_t == LANES - 1, lane_t == 0
-
-    def planes(cur, c, yt, first, last):
-        new = 1 - cur
-        y0 = pl.multiple_of(yt * TILE, TILE)
+    no_heat = jnp.zeros((TILE, LANES), jnp.float32)
+
+    def planes(par, y0, first, last):
+        old, new = F[par], F[1 - par]
+        y0 = pl.multiple_of(y0, TILE)
         rows = pl.ds(pl.multiple_of(y0 + TILE, TILE), TILE)
-
-        def temp(p, i, shift=0):
-            if shift:
-                return F[cur, p, 1 + c * NZ + i, pl.ds(y0 + TILE + shift, TILE), :]
-            return F[cur, p, 1 + c * NZ + i, rows, :]
-
-        def face_x(p, i):
-            return Gx[p, c * NZ + i, pl.ds(y0, TILE), :]
-
-        center = [temp(first, i) for i in range(NZ)]
-        below = [face_x(first - 1, i) * (center[i] - temp(first - 1, i)) for i in range(NZ)]
+        all_z = range(ZB)
+
+        def temp(p, zb, shift=0):
+            return old[p, zb, rows if shift == 0 else pl.ds(y0 + TILE + shift, TILE), :]
+
+        center = [temp(first, zb) for zb in all_z]
+        below = [Gx[first - 1, zb, pl.ds(y0, TILE), :] * (center[zb] - temp(first - 1, zb)) for zb in all_z]
         for p in range(first, last):
             xl = p - 1
-            ahead = [temp(p + 1, i) for i in range(NZ)]
-            above = [face_x(p, i) * (ahead[i] - center[i]) for i in range(NZ)]
-            line = [temp(p, -1)] + center + [temp(p, NZ)]
-            turned = [None] + [pltpu.roll(line[i], LANES - 1, 1) for i in range(1, NZ + 2)]
-            flow = [Gz[xl, c * NZ, pl.ds(y0, TILE), :] * (turned[1] - line[0])]
-            for i in range(1, NZ + 1):
-                up = jnp.where(top_lane, turned[i + 1], turned[i])
-                flow.append(Gz[xl, c * NZ + i, pl.ds(y0, TILE), :] * (up - line[i]))
-            moved = [pltpu.roll(flow[i], 1, 1) for i in range(NZ + 1)]
-            for i in range(NZ):
-                z_part = flow[i + 1] - jnp.where(low_lane, moved[i], moved[i + 1])
-                y_high = Gy[xl, c * NZ + i, rows, :] * (temp(p, i, 1) - center[i])
-                y_low = Gy[xl, c * NZ + i, pl.ds(y0 + TILE - 1, TILE), :] * (center[i] - temp(p, i, -1))
-                at = pl.multiple_of((xl * ZB + c * NZ + i) * SY + y0, TILE)
-                total = (above[i] - below[i]) + (y_high - y_low) + z_part
-                F[new, p, 1 + c * NZ + i, rows, :] = center[i] + (total + SRC[pl.ds(at, TILE), :])
+            ahead = [temp(p + 1, zb) for zb in all_z]
+            above = [Gx[p, zb, pl.ds(y0, TILE), :] * (ahead[zb] - center[zb]) for zb in all_z]
+            after = [pltpu.roll(now, LANES - 1, 1) for now in center] + [no_heat]
+            before = [no_heat] + [pltpu.roll(now, 1, 1) for now in center]
+            for zb in all_z:
+                now = center[zb]
+                z_high = GzH[xl, zb, pl.ds(y0, TILE), :] * (jnp.where(top_lane, after[zb + 1], after[zb]) - now)
+                z_low = GzL[xl, zb, pl.ds(y0, TILE), :] * (now - jnp.where(low_lane, before[zb], before[zb + 1]))
+                y_high = Gy[xl, zb, rows, :] * (temp(p, zb, 1) - now)
+                y_low = Gy[xl, zb, pl.ds(y0 + TILE - 1, TILE), :] * (now - temp(p, zb, -1))
+                at = pl.multiple_of((xl * ZB + zb) * SY + y0, TILE)
+                total = (above[zb] - below[zb]) + (y_high - y_low) + (z_high - z_low)
+                new[p, zb, rows, :] = now + (total + SRC[pl.ds(at, TILE), :])
             center, below = ahead, above
 
     def keep(cur, with_source):
@@ -608,7 +600,7 @@
             @pl.loop(0, ZB)
             def _(zb):
                 at = pl.ds(pl.multiple_of((xl * ZB + zb) * SY, SY), SY)
-                now = F[cur, 1 + xl, 1 + zb, pl.ds(TILE, SY), :]
+                now = F[cur][1 + xl, zb, pl.ds(TILE, SY), :]
                 FG[at, :] = now
                 if with_source:
                     SRC[at, :] = SRC[at, :] - W[at, :] * now
@@ -627,68 +619,101 @@
 
     total_sweeps = STEPS * SWEEPS
 
-    @pl.loop(0, total_sweeps)
-    def _(s):
-        cur = lax.rem(s, 2)
-        new = 1 - cur
+    def sweep(s, par):
+        new = 1 - par
+        more = s < total_sweeps - 1
 
         @pl.loop(0, NC)
-        def _(c):
-            at_each(gets_y, lambda way: y_copy(way, cur, c).wait_recv())
-            unpack_y(cur, c)
-            at_each(gets_x, lambda way: x_copy(way, cur, c).wait_recv())
+        def _(k):
+            c = jnp.where(k == 0, 0, jnp.where(k == 1, NC - 1, k - 1))
+            first, last = k == 0, k == 1
+
+            @pl.when(first)
+            def _():
+                @pl.when(has_down)
+                def _():
+                    y_copy(1, par).wait_recv()
+
+                unpack_y(par, 0)
+
+            @pl.when(last)
+            def _():
+                @pl.when(has_up)
+                def _():
+                    y_copy(0, par).wait_recv()
+
+                unpack_y(par, 1)
+
+            at_each(gets_x, lambda way: x_copy(way, par, c).wait_recv())
 
             @pl.when(s >= 1)
             def _():
                 at_each(sends_x, lambda way: x_copy(way, new, c).wait_send())
-                at_each(sends_y, lambda way: y_copy(way, new, c).wait_send())
-
-            @pl.loop(0, YT)
-            def _(yt):
-                planes(cur, c, yt, 1, 2)
-                planes(cur, c, yt, SX, SX + 1)
-
-            @pl.when(s < total_sweeps - 1)
+
+            @pl.loop(0, CY // TILE)
+            def _(i):
+                planes(par, c * CY + i * TILE, 1, 2)
+                planes(par, c * CY + i * TILE, SX, SX + 1)
+
+            @pl.when(more)
             def _():
                 at_each(sends_x, lambda way: x_copy(way, new, c).start())
 
-            @pl.loop(0, YT)
-            def _(yt):
-                planes(cur, c, yt, 2, SX)
-
-            @pl.when(s < total_sweeps - 1)
+            @pl.loop(0, CY // TILE)
+            def _(i):
+                planes(par, c * CY + i * TILE, 2, SX)
+
+            def send_y(way):
+                @pl.when(s >= 1)
+                def _():
+                    y_copy(way, new).wait_send()
+
+                @pl.when(more)
+                def _():
+                    pack_y(new, way)
+                    y_copy(way, new).start()
+
+            @pl.when(first & has_down)
             def _():
-                pack_y(new, c)
-                at_each(sends_y, lambda way: y_copy(way, new, c).start())
-
+                send_y(0)
+
+            @pl.when(last & has_up)
+            def _():
+                send_y(1)
+
+    @pl.loop(0, total_sweeps // 2)
+    def _(pair):
+        sweep(2 * pair, 0)
         half = (n_tool + 1) // 2
 
-        @pl.when(s == 0)
+        @pl.when(pair == 0)
         def _():
             send_all(msg2_copy, 1, half)
 
-        @pl.when(s == 1)
-        def _():
-            send_all(msg2_copy, half, n_tool)
-
-        @pl.when(s == 2)
+        @pl.when(pair == 1)
         def _():
             wait_arrivals(msg2_copy)
             split_rows(msg2r, CAP, 0, 0)
             split_rows(msg2r, CAP, CAP, 2 * LANES)
             scatter(0, to_weight)
 
-        @pl.when(s == SWEEPS - 1)
-        def _():
-            scatter(2 * LANES, to_source)
-            keep(new, True)
-
-        @pl.when(s == SWEEPS)
+        @pl.when(pair == 2)
         def _():
             collect(0)
             send_all(back_copy[0], 1, half)
 
-        @pl.when(s == SWEEPS + 1)
+        sweep(2 * pair + 1, 1)
+
+        @pl.when(pair == 0)
+        def _():
+            send_all(msg2_copy, half, n_tool)
+
+        @pl.when(pair == 1)
+        def _():
+            scatter(2 * LANES, to_source)
+            keep(0, True)
+
+        @pl.when(pair == 2)
         def _():
             send_all(back_copy[0], half, n_tool)
 
@@ -728,12 +753,11 @@
     at_each(sends_x, lambda way: kx_copy(way).wait_send())
     at_each(sends_y, lambda way: ky_copy(way).wait_send())
 
-    last = (total_sweeps - 1) % 2
-
     @pl.loop(0, NC)
     def _(c):
-        at_each(sends_x, lambda way: x_copy(way, last, c).wait_send())
-        at_each(sends_y, lambda way: y_copy(way, last, c).wait_send())
+        at_each(sends_x, lambda way: x_copy(way, 1, c).wait_send())
+
+    at_each(sends_y, lambda way: y_copy(way, 1).wait_send())
 
     for copy in stores:
         copy.wait()
@@ -745,7 +769,7 @@
 def on_device(n_tool, n_blank, tool_temp, material, conductivity, shell_temp, base_rate, film, contact_temp, pair_slab, pair_block, bead_ids, bead_gain):
     SX, SY, SZ = tool_temp.shape
     ZB = SZ // LANES
-    NC = ZB // NZ
+    NC = CHUNKS
     BLK = shell_temp.shape[0]
     beadrows = bead_ids.shape[0] // LANES
     slots = n_tool * CAP
@@ -754,12 +778,14 @@
     V = pltpu.VMEM
     dma = pltpu.SemaphoreType.DMA
     scratch = [
-        V((2, SX + 2, ZB + 2, SY + 2 * TILE, LANES), f32),
+        V((SX + 2, ZB, SY + 2 * TILE, LANES), f32),
+        V((SX + 2, ZB, SY + 2 * TILE, LANES), f32),
         V((SX + 2, ZB, SY + 2 * TILE, LANES), f32),
         V((SX, ZB, SY, LANES), i32),
         V((SX + 1, ZB, SY, LANES), f32),
         V((SX, ZB, SY + TILE, LANES), f32),
-        V((SX, ZB + 1, SY, LANES), f32),
+        V((SX, ZB, SY, LANES), f32),
+        V((SX, ZB, SY, LANES), f32),
         V((voxel_blocks, LANES), f32),
         V((voxel_blocks, LANES), f32),
         V((voxel_blocks, LANES), f32),
@@ -793,8 +819,8 @@
         dma,
         dma((2, 2, NC)),
         dma((2, 2, NC)),
-        dma((2, 2, NC)),
-        dma((2, 2, NC)),
+        dma((2, 2)),
+        dma((2, 2)),
         dma((2, 2)),
         dma((2, 2)),
         dma((n_tool,)),

time: 367 us -> 120 us (0.33)
  Pallas kernels: 361 us -> 114 us
    pallas_call x1, Pallas kernels: 361 us -> 114 us  [on_device(): pl.pallas_call(functools.partial(kernel, (n_tool, n_blank, SX, SY, ZB, BL...]
where the time goes in v2:
time: 120 us
  Pallas kernels  114 us (95%)
  local copies, waits for them, and re-layouts  4.63 us (4%)
    pallas_call x1, Pallas kernels, on_device(): pl.pallas_call(functools.partial(kernel, (n_tool, n_blank, SX, SY, ZB, BL...  114 us
    unnamed x7, local copies, waits for them, and re-layouts  4.63 us

profile of v2, /device:TPU:96, one launch (start us, length us, event | category | flops | bytes accessed | tf_op | source)
XLA Modules:
  0.0 119.6 jit_solution(7498879884247027011)
XLA Ops:
  0.6 114.3 %shard_map.130 = (f32[8,64,1024]{2,1,0:T(8,128)}, f32[512,128]{1,0:T(8,128)}, f32[512,128]{1,0:T(8,128)}) custom-call(f32[8,64,1024]{2,1,0:T(8,128)} %tool_hbm.1, s32[8,64,1024]{2,1,0:T(8,128)} %mat_hbm.1, f32[8]{0:T(128)} %cond.1, f32[512,128]{1,0:T(8,128)} %theta0.1, f32[512,128]{1,0:T(8,128)} %base_rate.1, f32[512,128]{1,0:T(8,128)} %film.1, ...), custom_call_target="tpu_custom_call" | custom-call | tf_op jit(solution)/shard_map/pallas_call | solution.py:837
  115.0 0.0 copy-start.1
  115.0 0.0 copy-start
  115.0 3.2 %copy.17 = f32[8,64,1024]{2,1,0:T(8,128)} copy(f32[8,64,1024]{2,1,0:T(8,128)} %get-tuple-element.6) | data formatting | bytes 4194304
  118.2 0.0 copy-done.1
  118.2 0.7 copy.18
  118.9 0.0 copy-done
  118.9 0.7 copy.19
Async XLA Ops:
  115.0 3.2 %copy-start.1 = (f32[512,128]{1,0:T(8,128)S(1)}, f32[512,128]{1,0:T(8,128)}, u32[]{:S(2)}) copy-start(f32[512,128]{1,0:T(8,128)} %get-tuple-element.7) | copy-start | bytes 786436
  115.0 3.9 %copy-start = (f32[512,128]{1,0:T(8,128)S(1)}, f32[512,128]{1,0:T(8,128)}, u32[]{:S(2)}) copy-start(f32[512,128]{1,0:T(8,128)} %get-tuple-element.8) | copy-start | bytes 786436

commit v3 on v2

--- a/solution.py
+++ b/solution.py
@@ -1,4 +1,5 @@
 import functools
+import math
 
 import jax
 import jax.numpy as jnp
@@ -66,6 +67,7 @@
     GzL,
     SRC,
     W,
+    BD,
     FG,
     O,
     PM,
@@ -87,8 +89,10 @@
     kyr,
     msg1s,
     msg1r,
-    msg2s,
-    msg2r,
+    msgWs,
+    msgWr,
+    msgBs,
+    msgBr,
     backs,
     backr,
     theta1,
@@ -105,8 +109,10 @@
     metars,
     m1ss,
     m1rs,
-    m2ss,
-    m2rs,
+    mWss,
+    mWrs,
+    mBss,
+    mBrs,
     bss,
     brs,
 ):
@@ -238,13 +244,41 @@
         total = lax.fori_loop(0, BLK // 16, part, jnp.zeros((TILE, LANES), jnp.int32), unroll=4)
         metas[q] = fold_rows(total) - 1
 
+    outflow = film[...] * (theta0[...] - contact[...])
+    hi, lo = split_pair(outflow)
+    XB[:, 0:LANES] = hi
+    XB[:, LANES : 2 * LANES] = lo
+    part_rows = min(512, slots)
+    step_rows = min(512, voxel_blocks)
+
+    def pack(write, columns):
+        @pl.loop(0, slots // part_rows)
+        def _(i):
+            got = jnp.dot(
+                PM[pl.ds(pl.multiple_of(i * part_rows, part_rows), part_rows), :],
+                XB[:, columns : columns + 2 * LANES],
+                preferred_element_type=jnp.float32,
+            )
+            rows = got[:, :LANES] + got[:, LANES:]
+            write(i * (part_rows // CAP), rows.reshape(part_rows // CAP, CAP, LANES))
+
+    def write1(d, rows):
+        msg1s[pl.ds(d, part_rows // CAP)] = rows
+
+    pack(write1, 0)
+
     pl.semaphore_wait(barrier, n_tool - 1 + jnp.where(has_down, 1, 0) + jnp.where(has_up, 1, 0))
 
-    def partner(off):
-        return lax.rem(t + off, n_tool)
-
-    def source_of(off):
-        return lax.rem(t + n_tool - off, n_tool)
+    side = math.isqrt(n_tool)
+    row, column = t // side, lax.rem(t, side)
+
+    def partner(k):
+        step = lax.rem(k * 7, n_tool)
+        return lax.rem(row + step // side, side) * side + lax.rem(column + lax.rem(step, side), side)
+
+    def source_of(k):
+        step = lax.rem(k * 7, n_tool)
+        return lax.rem(row + side - step // side, side) * side + lax.rem(column + side - lax.rem(step, side), side)
 
     def meta_copy(d, s):
         return pltpu.make_async_remote_copy(
@@ -270,7 +304,8 @@
         return make
 
     msg1_copy = row_copy(msg1s, msg1r, m1ss, m1rs)
-    msg2_copy = row_copy(msg2s, msg2r, m2ss, m2rs)
+    msgW_copy = row_copy(msgWs, msgWr, mWss, mWrs)
+    msgB_copy = row_copy(msgBs, msgBr, mBss, mBrs)
     back_copy = [
         row_copy(backs.at[k], backr.at[k], bss.at[k], brs.at[k]) for k in range(STEPS)
     ]
@@ -348,6 +383,11 @@
             def _(way=way):
                 act(way)
 
+    send_all(meta_copy, 1, n_tool)
+    send_all(msg1_copy, 1, n_tool)
+    metar[t] = metas[t // 2]
+    msg1r[t] = msg1s[t]
+
     for zb in range(ZB):
         loads[zb].wait()
 
@@ -371,33 +411,6 @@
 
     at_each(sends_y, lambda way: ky_copy(way).start())
 
-    outflow = film[...] * (theta0[...] - contact[...])
-    hi, lo = split_pair(outflow)
-    XB[:, 0:LANES] = hi
-    XB[:, LANES : 2 * LANES] = lo
-    part_rows = min(512, slots)
-    step_rows = min(512, voxel_blocks)
-
-    def pack(write, columns):
-        @pl.loop(0, slots // part_rows)
-        def _(i):
-            got = jnp.dot(
-                PM[pl.ds(pl.multiple_of(i * part_rows, part_rows), part_rows), :],
-                XB[:, columns : columns + 2 * LANES],
-                preferred_element_type=jnp.float32,
-            )
-            rows = got[:, :LANES] + got[:, LANES:]
-            write(i * (part_rows // CAP), rows.reshape(part_rows // CAP, CAP, LANES))
-
-    def write1(d, rows):
-        msg1s[pl.ds(d, part_rows // CAP)] = rows
-
-    pack(write1, 0)
-    send_all(meta_copy, 1, n_tool)
-    send_all(msg1_copy, 1, n_tool)
-    metar[t] = metas[t // 2]
-    msg1r[t] = msg1s[t]
-
     def pack_y(par, way):
         row = TILE if way == 0 else TILE + SY - 1
 
@@ -416,10 +429,6 @@
 
     for zb in range(ZB):
         loads[ZB + zb].wait()
-
-    @pl.loop(0, NC)
-    def _(c):
-        at_each(sends_x, lambda way: x_copy(way, 0, c).start())
 
     for way in range(2):
         pack_y(0, way)
@@ -459,12 +468,20 @@
     XB[:, 2 * LANES : 3 * LANES] = hi
     XB[:, 3 * LANES : 4 * LANES] = lo
 
-    def write2(d, rows, first):
-        msg2s[pl.ds(d, part_rows // CAP), first : first + CAP, :] = rows
-
-    pack(lambda d, rows: write2(d, rows, 0), 0)
-    pack(lambda d, rows: write2(d, rows, CAP), 2 * LANES)
-    msg2r[t] = msg2s[t]
+    def writeW(d, rows):
+        msgWs[pl.ds(d, part_rows // CAP)] = rows
+
+    def writeB(d, rows):
+        msgBs[pl.ds(d, part_rows // CAP)] = rows
+
+    pack(writeW, 0)
+    pack(writeB, 2 * LANES)
+    msgWr[t] = msgWs[t]
+    msgBr[t] = msgBs[t]
+
+    @pl.loop(0, NC)
+    def _(c):
+        at_each(sends_x, lambda way: x_copy(way, 0, c).start())
 
     lane = lax.broadcasted_iota(jnp.int32, (SY, LANES), 1)
     last_lane, first_lane = lane == LANES - 1, lane == 0
@@ -531,24 +548,20 @@
                 K[1 + xl, zb, pl.ds(TILE, SY), :] + K[1 + xl, zb, pl.ds(TILE + 1, SY), :]
             )
 
-    at_each(gets_x, lambda way: kx_copy(way).wait_recv())
-    x_faces(0)
-    x_faces(SX)
-
-    def split_rows(src, rows, first, column):
+    def split_rows(src):
         @pl.loop(0, n_tool)
         def _(s):
-            hi, lo = split_pair(src[s, first : first + rows, :])
+            hi, lo = split_pair(src[s])
             at = pl.ds(pl.multiple_of(s * CAP, CAP), CAP)
-            R[at, column : column + LANES] = hi
-            R[at, column + LANES : column + 2 * LANES] = lo
-
-    def scatter(column, write):
+            R[at, 0:LANES] = hi
+            R[at, LANES : 2 * LANES] = lo
+
+    def scatter(write):
         @pl.loop(0, voxel_blocks // step_rows)
         def _(m):
             at = pl.ds(pl.multiple_of(m * step_rows, step_rows), step_rows)
             got = jnp.dot(
-                O[at, :], R[:, column : column + 2 * LANES], preferred_element_type=jnp.float32
+                O[at, :], R[...], preferred_element_type=jnp.float32
             )
             write(at, source_step * (got[:, :LANES] + got[:, LANES:]))
 
@@ -558,15 +571,22 @@
     def to_weight(at, rows):
         W[at, :] = rows
 
+    def to_rest(at, rows):
+        BD[at, :] = rows
+
     wait_arrivals(msg1_copy)
-    split_rows(msg1r, CAP, 0, 0)
-    scatter(0, to_source)
+    split_rows(msg1r)
+    scatter(to_source)
+
+    at_each(gets_x, lambda way: kx_copy(way).wait_recv())
+    x_faces(0)
+    x_faces(SX)
 
     lane_t = lax.broadcasted_iota(jnp.int32, (TILE, LANES), 1)
     top_lane, low_lane = lane_t == LANES - 1, lane_t == 0
     no_heat = jnp.zeros((TILE, LANES), jnp.float32)
 
-    def planes(par, y0, first, last):
+    def planes(par, y0, first, last, final):
         old, new = F[par], F[1 - par]
         y0 = pl.multiple_of(y0, TILE)
         rows = pl.ds(pl.multiple_of(y0 + TILE, TILE), TILE)
@@ -591,37 +611,43 @@
                 y_low = Gy[xl, zb, pl.ds(y0 + TILE - 1, TILE), :] * (now - temp(p, zb, -1))
                 at = pl.multiple_of((xl * ZB + zb) * SY + y0, TILE)
                 total = (above[zb] - below[zb]) + (y_high - y_low) + (z_high - z_low)
-                new[p, zb, rows, :] = now + (total + SRC[pl.ds(at, TILE), :])
+                result = now + (total + SRC[pl.ds(at, TILE), :])
+                if final:
+                    FG[pl.ds(at, TILE), :] = result
+                else:
+                    new[p, zb, rows, :] = result
             center, below = ahead, above
 
-    def keep(cur, with_source):
+    def collect(k, d):
+        q = d // 2
+        lane0 = lax.rem(d, 2) * CAP
+
+        @pl.loop(0, CAP // TILE)
+        def _(j):
+            for i in range(TILE):
+                row = gidx_s[q, lane0 + j * TILE + i]
+                backs[k, d, pl.ds(pl.multiple_of(j * TILE, TILE) + i, 1), :] = FG[pl.ds(row, 1), :]
+
+    def collect_and_send(k):
+        @pl.loop(1, n_tool)
+        def _(off):
+            d = partner(off)
+            collect(k, d)
+            back_copy[k](d, t).start()
+
+        collect(k, t)
+
+    def next_source(c):
         @pl.loop(0, SX)
         def _(xl):
-            @pl.loop(0, ZB)
-            def _(zb):
-                at = pl.ds(pl.multiple_of((xl * ZB + zb) * SY, SY), SY)
-                now = F[cur][1 + xl, zb, pl.ds(TILE, SY), :]
+            for zb in range(ZB):
+                at = pl.ds(pl.multiple_of((xl * ZB + zb) * SY + c * CY, TILE), CY)
+                now = FA[1 + xl, zb, pl.ds(pl.multiple_of(TILE + c * CY, TILE), CY), :]
                 FG[at, :] = now
-                if with_source:
-                    SRC[at, :] = SRC[at, :] - W[at, :] * now
-
-    def collect(k):
-        @pl.loop(0, n_tool)
-        def _(s):
-            q = s // 2
-            lane0 = lax.rem(s, 2) * CAP
-
-            @pl.loop(0, CAP // TILE)
-            def _(j):
-                for i in range(TILE):
-                    row = gidx_s[q, lane0 + j * TILE + i]
-                    backs[k, s, pl.ds(pl.multiple_of(j * TILE, TILE) + i, 1), :] = FG[pl.ds(row, 1), :]
-
-    total_sweeps = STEPS * SWEEPS
-
-    def sweep(s, par):
+                SRC[at, :] = BD[at, :] - W[at, :] * now
+
+    def sweep(par, started=True, fresh=None, final=False):
         new = 1 - par
-        more = s < total_sweeps - 1
 
         @pl.loop(0, NC)
         def _(k):
@@ -644,32 +670,35 @@
 
                 unpack_y(par, 1)
 
+            if fresh is not None:
+                @pl.when(fresh)
+                def _():
+                    next_source(c)
+
             at_each(gets_x, lambda way: x_copy(way, par, c).wait_recv())
 
-            @pl.when(s >= 1)
+            @pl.when(started)
             def _():
                 at_each(sends_x, lambda way: x_copy(way, new, c).wait_send())
 
             @pl.loop(0, CY // TILE)
             def _(i):
-                planes(par, c * CY + i * TILE, 1, 2)
-                planes(par, c * CY + i * TILE, SX, SX + 1)
-
-            @pl.when(more)
-            def _():
+                planes(par, c * CY + i * TILE, 1, 2, final)
+                planes(par, c * CY + i * TILE, SX, SX + 1, final)
+
+            if not final:
                 at_each(sends_x, lambda way: x_copy(way, new, c).start())
 
             @pl.loop(0, CY // TILE)
             def _(i):
-                planes(par, c * CY + i * TILE, 2, SX)
+                planes(par, c * CY + i * TILE, 2, SX, final)
 
             def send_y(way):
-                @pl.when(s >= 1)
+                @pl.when(started)
                 def _():
                     y_copy(way, new).wait_send()
 
-                @pl.when(more)
-                def _():
+                if not final:
                     pack_y(new, way)
                     y_copy(way, new).start()
 
@@ -681,43 +710,36 @@
             def _():
                 send_y(1)
 
-    @pl.loop(0, total_sweeps // 2)
+    @pl.loop(0, STEPS * SWEEPS // 2 - 1)
     def _(pair):
-        sweep(2 * pair, 0)
-        half = (n_tool + 1) // 2
+        sweep(0, started=pair > 0, fresh=pair == 2)
 
         @pl.when(pair == 0)
         def _():
-            send_all(msg2_copy, 1, half)
+            send_all(msgW_copy, 1, n_tool)
 
         @pl.when(pair == 1)
         def _():
-            wait_arrivals(msg2_copy)
-            split_rows(msg2r, CAP, 0, 0)
-            split_rows(msg2r, CAP, CAP, 2 * LANES)
-            scatter(0, to_weight)
+            wait_arrivals(msgB_copy)
+            split_rows(msgBr)
+            scatter(to_rest)
 
         @pl.when(pair == 2)
         def _():
-            collect(0)
-            send_all(back_copy[0], 1, half)
-
-        sweep(2 * pair + 1, 1)
+            collect_and_send(0)
+
+        sweep(1)
 
         @pl.when(pair == 0)
         def _():
-            send_all(msg2_copy, half, n_tool)
-
-        @pl.when(pair == 1)
-        def _():
-            scatter(2 * LANES, to_source)
-            keep(0, True)
-
-        @pl.when(pair == 2)
-        def _():
-            send_all(back_copy[0], half, n_tool)
-
-    keep(0, False)
+            send_all(msgB_copy, 1, n_tool)
+            wait_arrivals(msgW_copy)
+            split_rows(msgWr)
+            scatter(to_weight)
+
+    sweep(0)
+    sweep(1, final=True)
+
     stores = [
         pltpu.make_async_copy(
             FG.at[pl.ds((xl * ZB + zb) * SY, SY), :],
@@ -727,16 +749,15 @@
         for xl in range(SX)
         for zb in range(ZB)
     ]
-    collect(1)
-    send_all(back_copy[1], 1, n_tool)
     for copy in stores:
         copy.start()
+    collect_and_send(1)
 
     def contact_of(k):
         backr[k, t] = backs[k, t]
         wait_arrivals(back_copy[k])
-        split_rows(backr.at[k], CAP, 0, 0)
-        got = jnp.dot(PT[...], R[:, 0 : 2 * LANES], preferred_element_type=jnp.float32)
+        split_rows(backr.at[k])
+        got = jnp.dot(PT[...], R[...], preferred_element_type=jnp.float32)
         return got[:, :LANES] + got[:, LANES:]
 
     flux = film[...] * (contact_of(0) - theta1[...])
@@ -747,7 +768,8 @@
 
     wait_sends(meta_copy)
     wait_sends(msg1_copy)
-    wait_sends(msg2_copy)
+    wait_sends(msgW_copy)
+    wait_sends(msgB_copy)
     wait_sends(back_copy[0])
     wait_sends(back_copy[1])
     at_each(sends_x, lambda way: kx_copy(way).wait_send())
@@ -789,11 +811,12 @@
         V((voxel_blocks, LANES), f32),
         V((voxel_blocks, LANES), f32),
         V((voxel_blocks, LANES), f32),
+        V((voxel_blocks, LANES), f32),
         V((voxel_blocks, slots), bf16),
         V((slots, BLK), bf16),
         V((BLK, slots), bf16),
         V((BLK, 4 * LANES), bf16),
-        V((slots, 4 * LANES), bf16),
+        V((slots, 2 * LANES), bf16),
         V((BLK, TILE * LANES), bf16),
         V((2 * LANES, TILE * LANES), bf16),
         V((BLK, 2 * LANES), f32),
@@ -809,8 +832,10 @@
         V((2, ZB, SX, LANES), f32),
         V((n_tool, CAP, LANES), f32),
         V((n_tool, CAP, LANES), f32),
-        V((n_tool, 2 * CAP, LANES), f32),
-        V((n_tool, 2 * CAP, LANES), f32),
+        V((n_tool, CAP, LANES), f32),
+        V((n_tool, CAP, LANES), f32),
+        V((n_tool, CAP, LANES), f32),
+        V((n_tool, CAP, LANES), f32),
         V((STEPS, n_tool, CAP, LANES), f32),
         V((STEPS, n_tool, CAP, LANES), f32),
         V((BLK, LANES), f32),
@@ -829,12 +854,14 @@
         dma((n_tool,)),
         dma((n_tool,)),
         dma((n_tool,)),
+        dma((n_tool,)),
+        dma((n_tool,)),
         dma((STEPS, n_tool)),
         dma((STEPS, n_tool)),
     ]
     whole = pl.BlockSpec(memory_space=pltpu.VMEM)
     far = pl.BlockSpec(memory_space=pl.ANY)
-    return pl.pallas_call(
+    results = pl.pallas_call(
         functools.partial(kernel, (n_tool, n_blank, SX, SY, ZB, BLK, beadrows)),
         out_shape=(
             jax.ShapeDtypeStruct(tool_temp.shape, f32),
@@ -861,6 +888,30 @@
         bead_gain.reshape(beadrows, LANES),
     )
 
+    return pl.pallas_call(
+        write_out,
+        out_shape=tuple(jax.ShapeDtypeStruct(r.shape, r.dtype) for r in results),
+        in_specs=[far] * 3,
+        out_specs=(far,) * 3,
+        scratch_shapes=[V(r.shape, f32) for r in results] + [dma((SX + 2,)), dma((SX + 2,))],
+        compiler_params=pltpu.CompilerParams(vmem_limit_bytes=60 * 2**20),
+    )(*results)
+
+
+def write_out(tool_in, shell_in, contact_in, tool_out, shell_out, contact_out, tool_held, shell_held, contact_held, in_sems, out_sems):
+    n = tool_in.shape[0]
+    parts = [(tool_in.at[i], tool_held.at[i], tool_out.at[i]) for i in range(n)]
+    parts += [(shell_in, shell_held, shell_out), (contact_in, contact_held, contact_out)]
+    reads = [pltpu.make_async_copy(src, held, in_sems.at[i]) for i, (src, held, _) in enumerate(parts)]
+    writes = [pltpu.make_async_copy(held, dst, out_sems.at[i]) for i, (_, held, dst) in enumerate(parts)]
+    for copy in reads:
+        copy.start()
+    for read, write in zip(reads, writes):
+        read.wait()
+        write.start()
+    for copy in writes:
+        copy.wait()
+
 
 def solution(mesh):
     placed = (

time: 120 us -> 114 us (0.950); the launches traced: 120 us -> 112 us
  local copies, waits for them, and re-layouts: 4.63 us -> 0 us
  Pallas kernels: 114 us -> 111 us
    pallas_call x1, Pallas kernels: 114 us -> 108 us  [on_device(): pl.pallas_call(functools.partial(kernel, (n_tool, n_blank, SX, SY, ZB, BL...]
    unnamed x7 -> x0, local copies, waits for them, and re-layouts: 4.63 us -> none
    pallas_call x0 -> x1, Pallas kernels: none -> 2.6 us  [on_device(): pl.pallas_call(write_out, out_shape=tuple((jax.ShapeDtypeStruct(r.shape,...]
where the time goes in v3:
time: 114 us; the launch traced here: 112 us
  Pallas kernels  111 us (97%)
    pallas_call x1, Pallas kernels, on_device(): pl.pallas_call(functools.partial(kernel, (n_tool, n_blank, SX, SY, ZB, BL...  108 us
    pallas_call x1, Pallas kernels, on_device(): pl.pallas_call(write_out, out_shape=tuple((jax.ShapeDtypeStruct(r.shape,...  2.6 us

profile of v3, /device:TPU:96, one launch (start us, length us, event | category | flops | bytes accessed | tf_op | source)
XLA Modules:
  0.0 111.7 jit_solution(9739239152372215084)
XLA Ops:
  0.6 108.5 %shard_map.130 = (f32[8,64,1024]{2,1,0:T(8,128)}, f32[512,128]{1,0:T(8,128)}, f32[512,128]{1,0:T(8,128)}) custom-call(f32[8,64,1024]{2,1,0:T(8,128)} %tool_hbm.1, s32[8,64,1024]{2,1,0:T(8,128)} %mat_hbm.1, f32[8]{0:T(128)} %cond.1, f32[512,128]{1,0:T(8,128)} %theta0.1, f32[512,128]{1,0:T(8,128)} %base_rate.1, f32[512,128]{1,0:T(8,128)} %film.1, ...), custom_call_target="tpu_custom_call" | custom-call | tf_op jit(solution)/shard_map/pallas_call | solution.py:864
  109.1 2.6 %shard_map.131 = (f32[8,64,1024]{2,1,0:T(8,128)}, f32[512,128]{1,0:T(8,128)}, f32[512,128]{1,0:T(8,128)}) custom-call(f32[8,64,1024]{2,1,0:T(8,128)} %get-tuple-element.6.tool_in, f32[512,128]{1,0:T(8,128)} %get-tuple-element.7.shell_in, f32[512,128]{1,0:T(8,128)} %get-tuple-element.8.contact_in), custom_call_target="tpu_custom_call" | custom-call | tf_op jit(solution)/shard_map/pallas_call | solution.py:891

commit v4 on v3

--- a/solution.py
+++ b/solution.py
@@ -45,6 +45,18 @@
     dims,
     tool_hbm,
     mat_hbm,
+    cond_hbm,
+    theta0_hbm,
+    base_hbm,
+    film_hbm,
+    contact_hbm,
+    slab_hbm,
+    block_hbm,
+    bead_hbm,
+    gain_hbm,
+    tool_out,
+    shell_out,
+    contact_out,
     cond,
     theta0,
     base_rate,
@@ -54,9 +66,8 @@
     block_rows,
     bead_rows,
     gain_rows,
-    tool_out,
-    shell_out,
-    contact_out,
+    shell_end,
+    contact_end,
     FA,
     FB,
     K,
@@ -96,8 +107,10 @@
     backs,
     backr,
     theta1,
+    in_sem,
     load_sem,
     out_sem,
+    end_sem,
     idx_sem,
     xss,
     xrs,
@@ -129,6 +142,38 @@
     has_left, has_right = t > 0, t < n_tool - 1
     has_down, has_up = b > 0, b < n_blank - 1
 
+    barrier = pltpu.get_barrier_semaphore()
+
+    @pl.loop(1, n_tool)
+    def _(off):
+        pl.semaphore_signal(
+            barrier, inc=1, device_id={"tool": lax.rem(t + off, n_tool)}, device_id_type=MESH
+        )
+
+    @pl.when(has_down)
+    def _():
+        pl.semaphore_signal(barrier, inc=1, device_id={"blank": b - 1}, device_id_type=MESH)
+
+    @pl.when(has_up)
+    def _():
+        pl.semaphore_signal(barrier, inc=1, device_id={"blank": b + 1}, device_id_type=MESH)
+
+    small = [
+        pltpu.make_async_copy(src, dst, in_sem.at[i])
+        for i, (src, dst) in enumerate(
+            (
+                (slab_hbm, slab_rows),
+                (block_hbm, block_rows),
+                (film_hbm, film),
+                (theta0_hbm, theta0),
+                (contact_hbm, contact),
+                (cond_hbm, cond),
+                (base_hbm, base_rate),
+                (bead_hbm, bead_rows),
+                (gain_hbm, gain_rows),
+            )
+        )
+    ]
     loads = []
     for zb in range(ZB):
         loads.append(
@@ -146,24 +191,9 @@
                 load_sem.at[0, zb],
             )
         )
-    for copy in loads:
+
+    for copy in small[:6] + loads + small[6:]:
         copy.start()
-
-    barrier = pltpu.get_barrier_semaphore()
-
-    @pl.loop(1, n_tool)
-    def _(off):
-        pl.semaphore_signal(
-            barrier, inc=1, device_id={"tool": lax.rem(t + off, n_tool)}, device_id_type=MESH
-        )
-
-    @pl.when(has_down)
-    def _():
-        pl.semaphore_signal(barrier, inc=1, device_id={"blank": b - 1}, device_id_type=MESH)
-
-    @pl.when(has_up)
-    def _():
-        pl.semaphore_signal(barrier, inc=1, device_id={"blank": b + 1}, device_id_type=MESH)
 
     def clear_plane(plane):
         @pl.loop(0, ZB)
@@ -201,6 +231,8 @@
     def row8(ref, g):
         return jnp.broadcast_to(ref[pl.ds(g, 1), :], (TILE, LANES))
 
+    for copy in small[:2]:
+        copy.wait()
     for g in range(groups):
         slot_col[pl.ds(g * LANES, LANES), :] = column_of(slab_rows[pl.ds(g, 1), :])
         blk = block_rows[pl.ds(g, 1), :]
@@ -244,6 +276,8 @@
         total = lax.fori_loop(0, BLK // 16, part, jnp.zeros((TILE, LANES), jnp.int32), unroll=4)
         metas[q] = fold_rows(total) - 1
 
+    for copy in small[2:5]:
+        copy.wait()
     outflow = film[...] * (theta0[...] - contact[...])
     hi, lo = split_pair(outflow)
     XB[:, 0:LANES] = hi
@@ -251,12 +285,12 @@
     part_rows = min(512, slots)
     step_rows = min(512, voxel_blocks)
 
-    def pack(write, columns):
+    def pack(write):
         @pl.loop(0, slots // part_rows)
         def _(i):
             got = jnp.dot(
                 PM[pl.ds(pl.multiple_of(i * part_rows, part_rows), part_rows), :],
-                XB[:, columns : columns + 2 * LANES],
+                XB[...],
                 preferred_element_type=jnp.float32,
             )
             rows = got[:, :LANES] + got[:, LANES:]
@@ -265,7 +299,7 @@
     def write1(d, rows):
         msg1s[pl.ds(d, part_rows // CAP)] = rows
 
-    pack(write1, 0)
+    pack(write1)
 
     pl.semaphore_wait(barrier, n_tool - 1 + jnp.where(has_down, 1, 0) + jnp.where(has_up, 1, 0))
 
@@ -388,6 +422,7 @@
     metar[t] = metas[t // 2]
     msg1r[t] = msg1s[t]
 
+    small[5].wait()
     for zb in range(ZB):
         loads[zb].wait()
 
@@ -433,51 +468,6 @@
     for way in range(2):
         pack_y(0, way)
     at_each(sends_y, lambda way: y_copy(way, 0).start())
-
-    for j in range(BEADROWS // TILE):
-        @pl.loop(0, TILE)
-        def _(i, j=j):
-            at = pl.ds(pl.multiple_of(i * LANES, LANES), LANES)
-            shell = bead_rows[pl.ds(j * TILE + i, 1), :]
-            row, lane = shell // LANES, shell % LANES
-            A[:, at] = one_hot(
-                lax.broadcasted_iota(jnp.int32, (BLK, LANES), 0) == jnp.broadcast_to(row, (BLK, LANES))
-            )
-            here = lax.broadcasted_iota(jnp.int32, (LANES, LANES), 0) == jnp.broadcast_to(lane, (LANES, LANES))
-            held = jnp.where(here, jnp.broadcast_to(gain_rows[pl.ds(j * TILE + i, 1), :], (LANES, LANES)), 0.0)
-            hi, lo = split_pair(held)
-            BT[0:LANES, at] = hi
-            BT[LANES : 2 * LANES, at] = lo
-
-        part = lax.dot_general(
-            A[...], BT[...], (((1,), (1,)), ((), ())), preferred_element_type=jnp.float32
-        )
-        if j == 0:
-            acc[...] = part
-        else:
-            acc[...] += part
-
-    sigma = 1.0 - 0.4 * jnp.tanh(theta0[...])
-    rate = base_rate[...] + sigma * (acc[:, :LANES] + acc[:, LANES:])
-    after = theta0[...] + shell_step * (sigma * rate - outflow)
-    theta1[...] = after
-    hi, lo = split_pair(film[...])
-    XB[:, 0:LANES] = hi
-    XB[:, LANES : 2 * LANES] = lo
-    hi, lo = split_pair(film[...] * after)
-    XB[:, 2 * LANES : 3 * LANES] = hi
-    XB[:, 3 * LANES : 4 * LANES] = lo
-
-    def writeW(d, rows):
-        msgWs[pl.ds(d, part_rows // CAP)] = rows
-
-    def writeB(d, rows):
-        msgBs[pl.ds(d, part_rows // CAP)] = rows
-
-    pack(writeW, 0)
-    pack(writeB, 2 * LANES)
-    msgWr[t] = msgWs[t]
-    msgBr[t] = msgBs[t]
 
     @pl.loop(0, NC)
     def _(c):
@@ -581,6 +571,49 @@
     at_each(gets_x, lambda way: kx_copy(way).wait_recv())
     x_faces(0)
     x_faces(SX)
+
+    def add_gains():
+        for copy in small[7:]:
+            copy.wait()
+        for j in range(BEADROWS // TILE):
+            @pl.loop(0, TILE)
+            def _(i, j=j):
+                at = pl.ds(pl.multiple_of(i * LANES, LANES), LANES)
+                shell = bead_rows[pl.ds(j * TILE + i, 1), :]
+                row, lane = shell // LANES, shell % LANES
+                A[:, at] = one_hot(
+                    lax.broadcasted_iota(jnp.int32, (BLK, LANES), 0) == jnp.broadcast_to(row, (BLK, LANES))
+                )
+                here = lax.broadcasted_iota(jnp.int32, (LANES, LANES), 0) == jnp.broadcast_to(lane, (LANES, LANES))
+                held = jnp.where(here, jnp.broadcast_to(gain_rows[pl.ds(j * TILE + i, 1), :], (LANES, LANES)), 0.0)
+                hi, lo = split_pair(held)
+                BT[0:LANES, at] = hi
+                BT[LANES : 2 * LANES, at] = lo
+
+            part = lax.dot_general(
+                A[...], BT[...], (((1,), (1,)), ((), ())), preferred_element_type=jnp.float32
+            )
+            if j == 0:
+                acc[...] = part
+            else:
+                acc[...] += part
+
+    def pack_pair(rows, out):
+        hi, lo = split_pair(rows)
+        XB[:, 0:LANES] = hi
+        XB[:, LANES : 2 * LANES] = lo
+
+        def write(d, rows):
+            out[pl.ds(d, part_rows // CAP)] = rows
+
+        pack(write)
+
+    def shells_after_first():
+        small[6].wait()
+        sigma = 1.0 - 0.4 * jnp.tanh(theta0[...])
+        rate = base_rate[...] + sigma * (acc[:, :LANES] + acc[:, LANES:])
+        outflow = film[...] * (theta0[...] - contact[...])
+        theta1[...] = theta0[...] + shell_step * (sigma * rate - outflow)
 
     lane_t = lax.broadcasted_iota(jnp.int32, (TILE, LANES), 1)
     top_lane, low_lane = lane_t == LANES - 1, lane_t == 0
@@ -628,14 +661,12 @@
                 row = gidx_s[q, lane0 + j * TILE + i]
                 backs[k, d, pl.ds(pl.multiple_of(j * TILE, TILE) + i, 1), :] = FG[pl.ds(row, 1), :]
 
-    def collect_and_send(k):
-        @pl.loop(1, n_tool)
+    def collect_and_send(k, first, last):
+        @pl.loop(first, last)
         def _(off):
             d = partner(off)
             collect(k, d)
             back_copy[k](d, t).start()
-
-        collect(k, t)
 
     def next_source(c):
         @pl.loop(0, SX)
@@ -716,7 +747,27 @@
 
         @pl.when(pair == 0)
         def _():
+            pack_pair(film[...], msgWs)
             send_all(msgW_copy, 1, n_tool)
+            msgWr[t] = msgWs[t]
+            add_gains()
+
+        @pl.when(pair == 1)
+        def _():
+            wait_arrivals(msgW_copy)
+            split_rows(msgWr)
+            scatter(to_weight)
+
+        @pl.when(pair == 2)
+        def _():
+            collect_and_send(0, 1, n_tool // 3 + 1)
+            collect(0, t)
+
+        sweep(1)
+
+        @pl.when(pair == 2)
+        def _():
+            collect_and_send(0, n_tool // 3 + 1, 2 * n_tool // 3 + 1)
 
         @pl.when(pair == 1)
         def _():
@@ -724,20 +775,15 @@
             split_rows(msgBr)
             scatter(to_rest)
 
-        @pl.when(pair == 2)
-        def _():
-            collect_and_send(0)
-
-        sweep(1)
-
         @pl.when(pair == 0)
         def _():
+            shells_after_first()
+            pack_pair(film[...] * theta1[...], msgBs)
             send_all(msgB_copy, 1, n_tool)
-            wait_arrivals(msgW_copy)
-            split_rows(msgWr)
-            scatter(to_weight)
+            msgBr[t] = msgBs[t]
 
     sweep(0)
+    collect_and_send(0, 2 * n_tool // 3 + 1, n_tool)
     sweep(1, final=True)
 
     stores = [
@@ -749,9 +795,10 @@
         for xl in range(SX)
         for zb in range(ZB)
     ]
+    collect_and_send(1, 1, n_tool)
+    collect(1, t)
     for copy in stores:
         copy.start()
-    collect_and_send(1)
 
     def contact_of(k):
         backr[k, t] = backs[k, t]
@@ -763,8 +810,12 @@
     flux = film[...] * (contact_of(0) - theta1[...])
     sigma = 1.0 - 0.4 * jnp.tanh(theta1[...])
     rate = base_rate[...] + sigma * (acc[:, :LANES] + acc[:, LANES:])
-    shell_out[...] = theta1[...] + shell_step * (flux + sigma * rate)
-    contact_out[...] = contact_of(1)
+    shell_end[...] = theta1[...] + shell_step * (flux + sigma * rate)
+    stores.append(pltpu.make_async_copy(shell_end, shell_out, end_sem.at[0]))
+    stores[-1].start()
+    contact_end[...] = contact_of(1)
+    stores.append(pltpu.make_async_copy(contact_end, contact_out, end_sem.at[1]))
+    stores[-1].start()
 
     wait_sends(meta_copy)
     wait_sends(msg1_copy)
@@ -800,6 +851,17 @@
     V = pltpu.VMEM
     dma = pltpu.SemaphoreType.DMA
     scratch = [
+        pltpu.SMEM(conductivity.shape, f32),
+        V((BLK, LANES), f32),
+        V((BLK, LANES), f32),
+        V((BLK, LANES), f32),
+        V((BLK, LANES), f32),
+        V((BLK // LANES, LANES), i32),
+        V((BLK // LANES, LANES), i32),
+        V((beadrows, LANES), i32),
+        V((beadrows, LANES), f32),
+        V((BLK, LANES), f32),
+        V((BLK, LANES), f32),
         V((SX + 2, ZB, SY + 2 * TILE, LANES), f32),
         V((SX + 2, ZB, SY + 2 * TILE, LANES), f32),
         V((SX + 2, ZB, SY + 2 * TILE, LANES), f32),
@@ -815,7 +877,7 @@
         V((voxel_blocks, slots), bf16),
         V((slots, BLK), bf16),
         V((BLK, slots), bf16),
-        V((BLK, 4 * LANES), bf16),
+        V((BLK, 2 * LANES), bf16),
         V((slots, 2 * LANES), bf16),
         V((BLK, TILE * LANES), bf16),
         V((2 * LANES, TILE * LANES), bf16),
@@ -839,8 +901,10 @@
         V((STEPS, n_tool, CAP, LANES), f32),
         V((STEPS, n_tool, CAP, LANES), f32),
         V((BLK, LANES), f32),
+        dma((9,)),
         dma((2, ZB)),
         dma((SX, ZB)),
+        dma((2,)),
         dma,
         dma((2, 2, NC)),
         dma((2, 2, NC)),
@@ -859,7 +923,6 @@
         dma((STEPS, n_tool)),
         dma((STEPS, n_tool)),
     ]
-    whole = pl.BlockSpec(memory_space=pltpu.VMEM)
     far = pl.BlockSpec(memory_space=pl.ANY)
     results = pl.pallas_call(
         functools.partial(kernel, (n_tool, n_blank, SX, SY, ZB, BLK, beadrows)),
@@ -868,8 +931,8 @@
             jax.ShapeDtypeStruct(shell_temp.shape, f32),
             jax.ShapeDtypeStruct(shell_temp.shape, f32),
         ),
-        in_specs=[far, far, pl.BlockSpec(memory_space=pltpu.SMEM)] + [whole] * 8,
-        out_specs=(far, whole, whole),
+        in_specs=[far] * 11,
+        out_specs=(far,) * 3,
         scratch_shapes=scratch,
         compiler_params=pltpu.CompilerParams(
             collective_id=0, has_side_effects=True, vmem_limit_bytes=60 * 2**20

time: 114 us -> 111 us (0.974)
  the two profiles are of different devices: /device:TPU:96 before, /device:TPU:72 now
where the time goes in v4:
time: 111 us
  Pallas kernels  110 us (99%)
    pallas_call x1, Pallas kernels, on_device(): pl.pallas_call(functools.partial(kernel, (n_tool, n_blank, SX, SY, ZB, BL...  107 us
    pallas_call x1, Pallas kernels, on_device(): pl.pallas_call(write_out, out_shape=tuple((jax.ShapeDtypeStruct(r.shape,...  2.6 us

profile of v4, /device:TPU:72, one launch (start us, length us, event | category | flops | bytes accessed | tf_op | source)
XLA Modules:
  0.0 110.6 jit_solution(18224555833790122755)
XLA Ops:
  0.6 107.3 %shard_map.130 = (f32[8,64,1024]{2,1,0:T(8,128)}, f32[512,128]{1,0:T(8,128)}, f32[512,128]{1,0:T(8,128)}) custom-call(f32[8,64,1024]{2,1,0:T(8,128)} %tool_hbm.1, s32[8,64,1024]{2,1,0:T(8,128)} %mat_hbm.1, f32[8]{0:T(128)} %cond_hbm.1, f32[512,128]{1,0:T(8,128)} %theta0_hbm.1, f32[512,128]{1,0:T(8,128)} %base_hbm.1, f32[512,128]{1,0:T(8,128)} %film_hbm.1, ...), custom_call_target="tpu_custom_call" | custom-call | tf_op jit(solution)/shard_map/pallas_call | solution.py:927
  108.0 2.6 %shard_map.131 = (f32[8,64,1024]{2,1,0:T(8,128)}, f32[512,128]{1,0:T(8,128)}, f32[512,128]{1,0:T(8,128)}) custom-call(f32[8,64,1024]{2,1,0:T(8,128)} %get-tuple-element.6.tool_in, f32[512,128]{1,0:T(8,128)} %get-tuple-element.7.shell_in, f32[512,128]{1,0:T(8,128)} %get-tuple-element.8.contact_in), custom_call_target="tpu_custom_call" | custom-call | tf_op jit(solution)/shard_map/pallas_call | solution.py:954

commit v5 on v4

--- a/solution.py
+++ b/solution.py
@@ -307,11 +307,11 @@
     row, column = t // side, lax.rem(t, side)
 
     def partner(k):
-        step = lax.rem(k * 7, n_tool)
+        step = k
         return lax.rem(row + step // side, side) * side + lax.rem(column + lax.rem(step, side), side)
 
     def source_of(k):
-        step = lax.rem(k * 7, n_tool)
+        step = k
         return lax.rem(row + side - step // side, side) * side + lax.rem(column + side - lax.rem(step, side), side)
 
     def meta_copy(d, s):

time: 111 us -> 106 us (0.955)
  the two profiles are of different devices: /device:TPU:72 before, /device:TPU:96 now
where the time goes in v5:
time: 106 us; the launch traced here: 105 us
  Pallas kernels  104 us (98%)
    pallas_call x1, Pallas kernels, on_device(): pl.pallas_call(functools.partial(kernel, (n_tool, n_blank, SX, SY, ZB, BL...  102 us
    pallas_call x1, Pallas kernels, on_device(): pl.pallas_call(write_out, out_shape=tuple((jax.ShapeDtypeStruct(r.shape,...  2.6 us

profile of v5, /device:TPU:96, one launch (start us, length us, event | category | flops | bytes accessed | tf_op | source)
XLA Modules:
  0.0 104.9 jit_solution(10222574269380515362)
XLA Ops:
  0.6 101.6 %shard_map.130 = (f32[8,64,1024]{2,1,0:T(8,128)}, f32[512,128]{1,0:T(8,128)}, f32[512,128]{1,0:T(8,128)}) custom-call(f32[8,64,1024]{2,1,0:T(8,128)} %tool_hbm.1, s32[8,64,1024]{2,1,0:T(8,128)} %mat_hbm.1, f32[8]{0:T(128)} %cond_hbm.1, f32[512,128]{1,0:T(8,128)} %theta0_hbm.1, f32[512,128]{1,0:T(8,128)} %base_hbm.1, f32[512,128]{1,0:T(8,128)} %film_hbm.1, ...), custom_call_target="tpu_custom_call" | custom-call | tf_op jit(solution)/shard_map/pallas_call | solution.py:927
  102.3 2.6 %shard_map.131 = (f32[8,64,1024]{2,1,0:T(8,128)}, f32[512,128]{1,0:T(8,128)}, f32[512,128]{1,0:T(8,128)}) custom-call(f32[8,64,1024]{2,1,0:T(8,128)} %get-tuple-element.6.tool_in, f32[512,128]{1,0:T(8,128)} %get-tuple-element.7.shell_in, f32[512,128]{1,0:T(8,128)} %get-tuple-element.8.contact_in), custom_call_target="tpu_custom_call" | custom-call | tf_op jit(solution)/shard_map/pallas_call | solution.py:954
